TPU v7x, 128 devices: a whole 4x4x4 slice. The times are simulated.
128 devices in a mesh: dp: 16 (over z, x), tensor: 8 (over y, core).
Axes of the slice: x: 4, y: 4, z: 4, core: 2. Of those that a mesh axis runs over, the one named last changes fastest.
Arguments:
- grad_gate: bfloat16 [16, 2048, 7168], P('dp', 'tensor'), may hold values from -6 to 6
- grad_up: bfloat16 [16, 2048, 7168], P('dp', 'tensor'), may hold values from -6 to 6
- err_gate: bfloat16 [16, 2048, 7168], P('dp', 'tensor'), may hold values from -4 to 4
- err_up: bfloat16 [16, 2048, 7168], P('dp', 'tensor'), may hold values from -4 to 4
- q_gate: float32 [7168, 64], replicated, may hold values from -0.0625 to 0.0625
- q_up: float32 [7168, 64], replicated, may hold values from -0.0625 to 0.0625
Outputs:
- new_err_gate: bfloat16 [16, 2048, 7168], P('dp', 'tensor')
- new_err_up: bfloat16 [16, 2048, 7168], P('dp', 'tensor')
- new_q_gate: float32 [7168, 64], replicated
- new_q_up: float32 [7168, 64], replicated
All inputs are finite; a program needn't handle non-finite values.
Results may differ from a plain program's by a relative error of at most 0.0013.
Values sent between devices are 32-bit elements; how exact they have to be, the bound alone decides.
A program may use at most 128 MiB of HBM per device.

v0:
```python
import jax
import jax.numpy as jnp
from jax import lax
from jax.sharding import PartitionSpec as P


def gram_of(left):
    return jnp.dot(
        left.T, left, precision=lax.Precision.HIGHEST, preferred_element_type=jnp.float32
    )


def orthonormal(left, gram):
    lower = jnp.linalg.cholesky(gram)
    return lax.linalg.triangular_solve(lower, left, left_side=False, lower=True, transpose_a=True)


def body(grad_gate, grad_up, err_gate, err_up, q_gate, q_up):
    hp = lax.Precision.HIGHEST
    mat_gate = grad_gate[0].astype(jnp.float32) + err_gate[0].astype(jnp.float32)
    mat_up = grad_up[0].astype(jnp.float32) + err_up[0].astype(jnp.float32)
    part_gate = jnp.dot(mat_gate, q_gate, precision=hp, preferred_element_type=jnp.float32)
    part_up = jnp.dot(mat_up, q_up, precision=hp, preferred_element_type=jnp.float32)
    left_gate, left_up = lax.psum((part_gate, part_up), "dp")
    gram_gate, gram_up = lax.psum((gram_of(left_gate), gram_of(left_up)), "tensor")
    ortho_gate = orthonormal(left_gate, gram_gate)
    ortho_up = orthonormal(left_up, gram_up)
    local_gate = jnp.einsum("rd,rk->dk", mat_gate, ortho_gate, precision=hp)
    local_up = jnp.einsum("rd,rk->dk", mat_up, ortho_up, precision=hp)
    summed_gate, summed_up = lax.psum((local_gate, local_up), ("dp", "tensor"))
    replicas = lax.axis_size("dp")
    new_q_gate = summed_gate / replicas
    new_q_up = summed_up / replicas
    new_err_gate = mat_gate - jnp.dot(
        ortho_gate, new_q_gate.T, precision=hp, preferred_element_type=jnp.float32
    )
    new_err_up = mat_up - jnp.dot(
        ortho_up, new_q_up.T, precision=hp, preferred_element_type=jnp.float32
    )
    return (
        new_err_gate.astype(jnp.bfloat16)[None],
        new_err_up.astype(jnp.bfloat16)[None],
        new_q_gate,
        new_q_up,
    )


def solution(mesh):
    placed = (
        P("dp", "tensor", None),
        P("dp", "tensor", None),
        P("dp", "tensor", None),
        P("dp", "tensor", None),
        P(),
        P(),
    )
    return jax.shard_map(
        body,
        mesh=mesh,
        in_specs=placed,
        out_specs=(P("dp", "tensor", None), P("dp", "tensor", None), P(), P()),
        check_vma=False,
    )
```

profile of v0, /device:TPU:1, one launch (start us, length us, event | category | flops | bytes accessed | tf_op | source)
XLA Modules:
  0.0 360.8 jit_solution(3118681278196450509)
XLA Ops:
  7.2 0.0 copy-start
  7.2 0.0 all-reduce.8.cloned.1.call-start
  7.2 1.4 copy-done
  8.7 0.0 copy-start.1
  8.7 0.0 copy-start.4
  8.7 0.0 copy-start.11
  8.7 10.1 %fusion.10 = f32[256,64]{0,1:T(8,128)} fusion(f32[7168,64]{0,1:T(8,128)S(1)} %copy-done, bf16[1,256,7168]{2,1,0:T(8,128)(2,1)} %param.11, bf16[1,256,7168]{2,1,0:T(8,128)(2,1)} %param.9), kind=kOutput, calls=%fused_computation.12 | convolution fusion | flops 1414791168 | bytes 9240576 | tf_op jit(solution)/shard_map/dot_general | solution.py:22
  18.7 0.0 copy-done.1
  18.7 0.0 copy-done.4
  18.7 0.0 copy-done.11
  18.7 7.7 %fusion.6 = f32[256,64]{0,1:T(8,128)} fusion(f32[7168,64]{0,1:T(8,128)S(1)} %copy-done.11, bf16[1,256,7168]{2,1,0:T(8,128)(2,1)S(1)} %copy-done.1, bf16[1,256,7168]{2,1,0:T(8,128)(2,1)S(1)} %copy-done.4), kind=kOutput, calls=%fused_computation.8 | convolution fusion | flops 1414791168 | bytes 9240576 | tf_op jit(solution)/shard_map/dot_general | solution.py:23
  26.4 0.0 all-reduce.8.cloned.1.call-update
  26.5 0.0 all-reduce.6.cloned.1.call-start
  26.5 84.6 %all-reduce.8.cloned.1.call-done = (f32[256,64]{0,1:T(8,128)}, f32[256,64]{0,1:T(8,128)}) async-done(((f32[256,64]{0,1:T(8,128)}, f32[256,64]{0,1:T(8,128)}), (f32[256,64]{0,1:T(8,128)}, f32[256,64]{0,1:T(8,128)})) %all-reduce.8.cloned.1.call-update) | async-done | bytes 131088 | tf_op jit(solution)/shard_map/psum | solution.py:24
  111.1 1.1 fusion.18
  112.2 1.1 fusion.19
  113.3 23.4 %all-reduce.2 = (f32[64,64]{0,1:T(8,128)S(1)}, f32[64,64]{0,1:T(8,128)S(1)}) all-reduce(f32[64,64]{0,1:T(8,128)S(1)} %fusion.18, f32[64,64]{0,1:T(8,128)S(1)} %fusion.19), channel_id=1, replica_groups=mesh['dp'=16,'tensor'=8] {'tensor'}, use_global_device_ids=true, to_apply=%region_1.0 | all-reduce | flops 8192 | bytes 65536 | tf_op jit(solution)/shard_map/psum | solution.py:25
  136.7 0.1 copy.11
  136.8 0.1 copy.13
  136.9 5.8 %cholesky.55 = f32[64,64]{1,0:T(8,128)S(1)} custom-call(f32[64,64]{1,0:T(8,128)S(1)} %get-tuple-element.12), custom_call_target="Cholesky" | custom-call | tf_op jit(solution)/shard_map/jit(cholesky)/cholesky | solution.py:14
  142.8 0.6 compare_reduce_fusion
  143.4 0.7 fusion.13
  144.1 4.9 %custom-call.7 = f32[1,64,64]{1,2,0:T(8,128)S(1)} custom-call(f32[1,64,64]{2,1,0:T(8,128)S(1)} %fusion.13), custom_call_target="InvertDiagBlocksLowerTriangular" | custom-call | tf_op jit(solution)/shard_map/triangular_solve/custom-call.0 | solution.py:15
  149.0 1.1 convolution_bitcast_fusion
  150.1 5.8 %cholesky.44 = f32[64,64]{1,0:T(8,128)S(1)} custom-call(f32[64,64]{1,0:T(8,128)S(1)} %get-tuple-element.13), custom_call_target="Cholesky" | custom-call | tf_op jit(solution)/shard_map/jit(cholesky)/cholesky | solution.py:14
  156.0 0.6 compare_reduce_fusion.1
  156.6 0.7 fusion.12
  157.3 4.9 %custom-call.6 = f32[1,64,64]{1,2,0:T(8,128)S(1)} custom-call(f32[1,64,64]{2,1,0:T(8,128)S(1)} %fusion.12), custom_call_target="InvertDiagBlocksLowerTriangular" | custom-call | tf_op jit(solution)/shard_map/triangular_solve/custom-call.0 | solution.py:15
  162.2 1.1 convolution_bitcast_fusion.1
  163.3 0.0 copy-start.2
  163.3 0.0 copy-start.5
  163.3 10.0 %fusion.8 = f32[7168,64]{0,1:T(8,128)} fusion(f32[256,64]{0,1:T(8,128)S(1)} %convolution_bitcast_fusion.1, bf16[1,256,7168]{2,1,0:T(8,128)(2,1)} %param.11, bf16[1,256,7168]{2,1,0:T(8,128)(2,1)} %param.9), kind=kOutput, calls=%fused_computation.10 | convolution fusion | flops 1414791168 | bytes 9240576 | tf_op jit(solution)/shard_map/rd,rk->dk/dot_general | solution.py:28
  173.3 0.0 copy-done.2
  173.3 0.0 copy-done.5
  173.3 6.9 %fusion.4 = f32[7168,64]{0,1:T(8,128)} fusion(f32[256,64]{0,1:T(8,128)S(1)} %convolution_bitcast_fusion, bf16[1,256,7168]{2,1,0:T(8,128)(2,1)S(1)} %copy-done.2, bf16[1,256,7168]{2,1,0:T(8,128)(2,1)S(1)} %copy-done.5), kind=kOutput, calls=%fused_computation.6 | convolution fusion | flops 1414791168 | bytes 9240576 | tf_op jit(solution)/shard_map/rd,rk->dk/dot_general | solution.py:29
  180.2 0.0 all-reduce.6.cloned.1.call-update
  180.2 152.6 %all-reduce.6.cloned.1.call-done = (f32[7168,64]{0,1:T(8,128)}, f32[7168,64]{0,1:T(8,128)}) async-done(((f32[7168,64]{0,1:T(8,128)}, f32[7168,64]{0,1:T(8,128)}), (f32[7168,64]{0,1:T(8,128)}, f32[7168,64]{0,1:T(8,128)})) %all-reduce.6.cloned.1.call-update) | async-done | bytes 3670032 | tf_op jit(solution)/shard_map/psum | solution.py:30
  332.8 0.0 copy-start.3
  332.8 0.0 copy-start.6
  332.8 1.8 broadcast_multiply_fusion.1
  334.6 0.0 copy-start.9
  334.6 3.1 broadcast_multiply_fusion
  337.7 0.0 copy-done.3
  337.7 0.0 copy-done.6
  337.7 0.0 copy-start.10
  337.7 0.0 copy-start.7
  337.7 0.0 copy-start.8
  337.7 8.1 %fusion.2 = bf16[1,256,7168]{2,1,0:T(8,128)(2,1)} fusion(f32[256,64]{0,1:T(8,128)S(1)} %convolution_bitcast_fusion, f32[7168,64]{0,1:T(8,128)S(1)} %broadcast_multiply_fusion, bf16[1,256,7168]{2,1,0:T(8,128)(2,1)S(1)} %copy-done.3, bf16[1,256,7168]{2,1,0:T(8,128)(2,1)S(1)} %copy-done.6), kind=kOutput, calls=%fused_computation.4 | convolution fusion | flops 1418461184 | bytes 12910592 | tf_op jit(solution)/shard_map/dot_general | solution.py:37
  345.8 0.0 copy-done.9
  345.8 0.0 copy-done.10
  345.8 0.0 copy-done.7
  345.8 0.0 copy-done.8
  345.8 8.1 %fusion.3 = bf16[1,256,7168]{2,1,0:T(8,128)(2,1)} fusion(f32[256,64]{0,1:T(8,128)S(1)} %convolution_bitcast_fusion.1, f32[7168,64]{0,1:T(8,128)S(1)} %broadcast_multiply_fusion.1, bf16[1,256,7168]{2,1,0:T(8,128)(2,1)S(1)} %copy-done.7, bf16[1,256,7168]{2,1,0:T(8,128)(2,1)S(1)} %copy-done.8), kind=kOutput, calls=%fused_computation.5 | convolution fusion | flops 1418461184 | bytes 12910592 | tf_op jit(solution)/shard_map/dot_general | solution.py:34
  (3 shorter events, 0.1 us)
Async XLA Ops:
  7.2 1.5 copy-start
  7.2 103.9 %all-reduce.8.cloned.1.call-start = ((), (), s32[]{:S(2)}) async-start(), calls=%async_computation.1 | async-start | bytes 262144 | tf_op jit(solution)/shard_map/psum | solution.py:24
  8.7 10.1 %copy-start.1 = (bf16[1,256,7168]{2,1,0:T(8,128)(2,1)S(1)}, bf16[1,256,7168]{2,1,0:T(8,128)(2,1)}, u32[]{:S(2)}) copy-start(bf16[1,256,7168]{2,1,0:T(8,128)(2,1)} %param.12) | copy-start | bytes 11010052
  8.7 10.1 %copy-start.4 = (bf16[1,256,7168]{2,1,0:T(8,128)(2,1)S(1)}, bf16[1,256,7168]{2,1,0:T(8,128)(2,1)}, u32[]{:S(2)}) copy-start(bf16[1,256,7168]{2,1,0:T(8,128)(2,1)} %param.10) | copy-start | bytes 11010052
  8.7 10.1 %copy-start.11 = (f32[7168,64]{0,1:T(8,128)S(1)}, f32[7168,64]{0,1:T(8,128)}, u32[]{:S(2)}) copy-start(f32[7168,64]{0,1:T(8,128)} %param.14) | copy-start | bytes 5505028
  26.5 306.3 %all-reduce.6.cloned.1.call-start = ((), (), s32[]{:S(2)}) async-start(), calls=%async_computation | async-start | bytes 7340032 | tf_op jit(solution)/shard_map/psum | solution.py:30
  163.3 10.0 %copy-start.2 = (bf16[1,256,7168]{2,1,0:T(8,128)(2,1)S(1)}, bf16[1,256,7168]{2,1,0:T(8,128)(2,1)}, u32[]{:S(2)}) copy-start(bf16[1,256,7168]{2,1,0:T(8,128)(2,1)} %param.12) | copy-start | bytes 11010052
  163.3 10.0 %copy-start.5 = (bf16[1,256,7168]{2,1,0:T(8,128)(2,1)S(1)}, bf16[1,256,7168]{2,1,0:T(8,128)(2,1)}, u32[]{:S(2)}) copy-start(bf16[1,256,7168]{2,1,0:T(8,128)(2,1)} %param.10) | copy-start | bytes 11010052
  332.8 4.9 %copy-start.3 = (bf16[1,256,7168]{2,1,0:T(8,128)(2,1)S(1)}, bf16[1,256,7168]{2,1,0:T(8,128)(2,1)}, u32[]{:S(2)}) copy-start(bf16[1,256,7168]{2,1,0:T(8,128)(2,1)} %param.12) | copy-start | bytes 11010052
  332.8 4.9 %copy-start.6 = (bf16[1,256,7168]{2,1,0:T(8,128)(2,1)S(1)}, bf16[1,256,7168]{2,1,0:T(8,128)(2,1)}, u32[]{:S(2)}) copy-start(bf16[1,256,7168]{2,1,0:T(8,128)(2,1)} %param.10) | copy-start | bytes 11010052
  334.6 11.3 %copy-start.9 = (f32[7168,64]{0,1:T(8,128)}, f32[7168,64]{0,1:T(8,128)S(1)}, u32[]{:S(2)}) copy-start(f32[7168,64]{0,1:T(8,128)S(1)} %broadcast_multiply_fusion.1) | copy-start | bytes 5505028
  337.7 8.1 %copy-start.10 = (f32[7168,64]{0,1:T(8,128)}, f32[7168,64]{0,1:T(8,128)S(1)}, u32[]{:S(2)}) copy-start(f32[7168,64]{0,1:T(8,128)S(1)} %broadcast_multiply_fusion) | copy-start | bytes 5505028
  337.7 8.1 %copy-start.7 = (bf16[1,256,7168]{2,1,0:T(8,128)(2,1)S(1)}, bf16[1,256,7168]{2,1,0:T(8,128)(2,1)}, u32[]{:S(2)}) copy-start(bf16[1,256,7168]{2,1,0:T(8,128)(2,1)} %param.11) | copy-start | bytes 11010052
  337.7 8.1 %copy-start.8 = (bf16[1,256,7168]{2,1,0:T(8,128)(2,1)S(1)}, bf16[1,256,7168]{2,1,0:T(8,128)(2,1)}, u32[]{:S(2)}) copy-start(bf16[1,256,7168]{2,1,0:T(8,128)(2,1)} %param.9) | copy-start | bytes 11010052
Sparse Core Ops, SparseCore 0:
  26.6 84.4 all-reduce.7
  180.3 152.4 all-reduce.5
where the time goes:
time: 361 us
  waiting for transfers between devices  237 us (66%)
  matrix products  55.3 us (15%)
  other arithmetic  29 us (8%)
  blocking collectives  23.4 us (6%)
  between operations  14.2 us (4%)
    psum x1, waiting for transfers between devices, body(): summed_gate, summed_up = lax.psum((local_gate, local_up), ('dp', 'tensor'))  153 us
    psum x1, waiting for transfers between devices, body(): left_gate, left_up = lax.psum((part_gate, part_up), 'dp')  84.6 us
    psum x1, blocking collectives, body(): lax.psum((gram_of(left_gate), gram_of(left_up)), 'tensor')  23.4 us
    another operation x6, other arithmetic, orthonormal(): lower = jnp.linalg.cholesky(gram)  13 us
    another operation x4, other arithmetic, orthonormal(): lax.linalg.triangular_solve(lower, left, left_side=False, lower=True, tra...  11.1 us
    dot_general x1, matrix products, body(): jnp.dot(mat_gate, q_gate, precision=hp, preferred_element_type=jnp.float32)  10.1 us
    dot_general x1, matrix products, body(): local_gate = jnp.einsum('rd,rk->dk', mat_gate, ortho_gate, precision=hp)  9.96 us
    dot_general x1, matrix products, body(): jnp.dot(ortho_gate, new_q_gate.T, precision=hp, preferred_element_type=jn...  8.12 us
  transfers between devices with their start and end apart: 2, of which 2 were waited for; matrix products, arithmetic and copies ran while one was open for 0% of the time, Pallas kernels for 0%

commit v1 on v0

v1 whole, which is shorter than its diff:
```python
import functools

import jax
import jax.numpy as jnp
from jax import lax
from jax.experimental import pallas as pl
from jax.experimental.pallas import tpu as pltpu
from jax.sharding import PartitionSpec as P

MESH = pl.DeviceIdType.MESH
F32 = jnp.float32
BF16 = jnp.bfloat16
HP = lax.Precision.HIGHEST

DP = 16
TENSOR = 8
D = 7168
ROWS = 256
RANK = 64
HALF = D // 2
CHUNKS = 4
CHUNK = D // CHUNKS
TILE = 256
PARTS = ((0, 1280), (1280, 1280), (2560, 1024))
STAGES = 7
CORE_SUM, A_SUM, B_SUM, C_SUM, B_ALL, A_ALL, CORE_ALL = range(STAGES)


def three(value):
    first = value.astype(BF16)
    rest = value - first.astype(F32)
    second = rest.astype(BF16)
    third = (rest - second.astype(F32)).astype(BF16)
    return first, second, third


def nt(left, right, precision=None):
    return lax.dot_general(
        left, right, (((1,), (1,)), ((), ())), precision=precision, preferred_element_type=F32
    )


def nn(left, right, precision=None):
    return jnp.dot(left, right, precision=precision, preferred_element_type=F32)


def exchange_kernel(
    grad_gate, err_gate, grad_up, err_up, q_gate, q_up,
    data, total, left, inverse,
    q_buf, p_acc, p_part, p_recv, p_stack, w_send, w_own, w_recv,
    a_recv0, a_recv1, a_recv2, a_sum0, a_sum1, a_sum2,
    b_recv0, b_recv1, b_recv2, c_recv0, c_recv1, c_recv2,
    g_part, g_recv, g_all, work, low,
    load_sem, p_send_sem, p_recv_sem, g_send_sem, g_recv_sem, w_send_sem, w_recv_sem,
):
    a_recv = (a_recv0, a_recv1, a_recv2)
    a_sum = (a_sum0, a_sum1, a_sum2)
    b_recv = (b_recv0, b_recv1, b_recv2)
    c_recv = (c_recv0, c_recv1, c_recv2)
    dp = lax.axis_index("dp")
    t = lax.axis_index("tensor")
    z, x = dp // 4, lax.rem(dp, 4)
    y, core = t // 2, lax.rem(t, 2)
    at = (x, y, z)

    def peer(axis, v):
        px, py, pz = (v if axis == i else at[i] for i in range(3))
        return (pz * 4 + px, py * 2 + core)

    def send(src, dst, send_sem, recv_sem, device):
        pltpu.make_async_remote_copy(
            src_ref=src, dst_ref=dst, send_sem=send_sem, recv_sem=recv_sem,
            device_id=device, device_id_type=MESH,
        ).start()

    def arrived(ref, sem):
        pltpu.make_async_copy(ref, ref, sem).wait()

    sources = ((q_gate, grad_gate, err_gate), (q_up, grad_up, err_up))

    def load(g, c, k):
        cols = pl.ds(c * CHUNK, CHUNK)
        if k == 0:
            dst = q_buf.at[g, :, cols]
        else:
            dst = data.at[pl.ds((2 * g + k - 1) * ROWS, ROWS), cols]
        return pltpu.make_async_copy(sources[g][k].at[:, cols], dst, load_sem.at[g, c, k])

    for g in range(2):
        for c in range(CHUNKS):
            for k in range(3):
                load(g, c, k).start()

    barrier = pltpu.get_barrier_semaphore()
    for d in range(1, DP):
        pl.semaphore_signal(
            barrier, inc=1, device_id=(lax.rem(dp + d, DP), t), device_id_type=MESH
        )
    for d in range(1, TENSOR):
        pl.semaphore_signal(
            barrier, inc=1, device_id=(dp, lax.rem(t + d, TENSOR)), device_id_type=MESH
        )

    def chunk_of(member):
        return pl.ds(pl.multiple_of(8 * (member // 2), 8), 8), pl.ds(
            pl.multiple_of(128 * lax.rem(member, 2), 128), 128
        )

    def p_compute(g):
        for c in range(CHUNKS):
            for k in range(3):
                load(g, c, k).wait()
            q3 = jnp.concatenate(three(q_buf[g, :, c * CHUNK : (c + 1) * CHUNK]), axis=0)
            both = nt(data[2 * g * ROWS : (2 * g + 2) * ROWS, c * CHUNK : (c + 1) * CHUNK], q3)
            if c == 0:
                p_acc[...] = both
            else:
                p_acc[...] += both
        both = p_acc[:ROWS, :] + p_acc[ROWS:, :]
        turned = both.T
        p_part[g] = turned[:RANK] + turned[RANK : 2 * RANK] + turned[2 * RANK :]

    def p_sum_start(g):
        for d in range(1, DP):
            member = lax.rem(dp + d, DP)
            rows, cols = chunk_of(member)
            send(
                p_part.at[g, rows, cols], p_recv.at[g, d - 1],
                p_send_sem.at[g, 0], p_recv_sem.at[g, 0], (member, t),
            )

    def p_all_start(g):
        arrived(p_recv.at[g], p_recv_sem.at[g, 0])
        rows, cols = chunk_of(dp)
        summed = p_part[g, rows, cols]
        for d in range(DP - 1):
            summed = summed + p_recv[g, d]
        left[g, rows, cols] = summed
        for d in range(1, DP):
            send(
                left.at[g, rows, cols], left.at[g, rows, cols],
                p_send_sem.at[g, 1], p_recv_sem.at[g, 1], (lax.rem(dp + d, DP), t),
            )

    def p_done(g):
        arrived(p_recv.at[g], p_recv_sem.at[g, 1])
        p3 = jnp.concatenate(three(left[g]), axis=0)
        p_stack[g, :, :ROWS] = p3
        p_stack[g, :, ROWS:] = p3

    def w_block(g, dst, half, p):
        first, width = PARTS[p]
        start = pl.multiple_of(half * HALF + first, 128)

        def step(i, carry):
            offset = pl.multiple_of(i * TILE, TILE)
            cols = pl.ds(pl.multiple_of(start + offset, 128), TILE)
            prod = nn(p_stack[g], data[pl.ds(2 * g * ROWS, 2 * ROWS), cols])
            dst[g, :, pl.ds(pl.multiple_of(first + offset, 128), TILE)] = (
                prod[:RANK] + prod[RANK : 2 * RANK] + prod[2 * RANK :]
            )
            return carry

        lax.fori_loop(0, width // TILE, step, 0)

    def sems(g, p, stage):
        return w_send_sem.at[g, p, stage], w_recv_sem.at[g, p, stage]

    def axes_of(g, p):
        first = (p + g) % 3
        return first, (first + 1) % 3, (first + 2) % 3

    def part_cols(p):
        return pl.ds(PARTS[p][0], PARTS[p][1])

    def total_block(g, p):
        a, _, _ = axes_of(g, p)
        first, width = PARTS[p]
        return total.at[
            g,
            pl.ds(pl.multiple_of(16 * at[a], 16), 16),
            pl.ds(pl.multiple_of(core * HALF + first, 128), width),
        ]

    def total_leaf(g, p):
        a, b, _ = axes_of(g, p)
        first, width = PARTS[p]
        row = 16 * at[a] + 8 * (at[b] // 2)
        col = core * HALF + first + (width // 2) * lax.rem(at[b], 2)
        return total.at[
            g, pl.ds(pl.multiple_of(row, 8), 8), pl.ds(pl.multiple_of(col, 128), width // 2)
        ]

    def core_start(g):
        for p in range(3):
            w_block(g, w_send, 1 - core, p)
            send(
                w_send.at[g, :, part_cols(p)], w_recv.at[g, :, part_cols(p)],
                *sems(g, p, CORE_SUM), (dp, y * 2 + 1 - core),
            )

    def a_start(g):
        for p in range(3):
            w_block(g, w_own, core, p)
            first, width = PARTS[p]
            cols = part_cols(p)
            arrived(w_recv.at[g, :, cols], w_recv_sem.at[g, p, CORE_SUM])
            w_own[g, :, cols] += w_recv[g, :, cols]
            a, _, _ = axes_of(g, p)
            for d in range(1, 4):
                v = lax.rem(at[a] + d, 4)
                send(
                    w_own.at[g, pl.ds(pl.multiple_of(16 * v, 16), 16), cols],
                    a_recv[p].at[g, d - 1],
                    *sems(g, p, A_SUM), peer(a, v),
                )

    def b_start(g):
        for p in range(3):
            a, b, _ = axes_of(g, p)
            first, width = PARTS[p]
            arrived(a_recv[p].at[g], w_recv_sem.at[g, p, A_SUM])
            a_sum[p][g] = (
                w_own[g, pl.ds(pl.multiple_of(16 * at[a], 16), 16), part_cols(p)]
                + a_recv[p][g, 0] + a_recv[p][g, 1] + a_recv[p][g, 2]
            )
            for d in range(1, 4):
                v = lax.rem(at[b] + d, 4)
                send(
                    a_sum[p].at[g, leaf_rows(v), leaf_cols(v, width)], b_recv[p].at[g, d - 1],
                    *sems(g, p, B_SUM), peer(b, v),
                )

    def leaf_rows(v):
        return pl.ds(pl.multiple_of(8 * (v // 2), 8), 8)

    def leaf_cols(v, width):
        return pl.ds(pl.multiple_of((width // 2) * lax.rem(v, 2), 128), width // 2)

    def c_start(g):
        for p in range(3):
            _, b, c = axes_of(g, p)
            first, width = PARTS[p]
            arrived(b_recv[p].at[g], w_recv_sem.at[g, p, B_SUM])
            c_recv[p][g, at[c]] = (
                a_sum[p][g, leaf_rows(at[b]), leaf_cols(at[b], width)]
                + b_recv[p][g, 0] + b_recv[p][g, 1] + b_recv[p][g, 2]
            )
            for d in range(1, 4):
                send(
                    c_recv[p].at[g, at[c]], c_recv[p].at[g, at[c]],
                    *sems(g, p, C_SUM), peer(c, lax.rem(at[c] + d, 4)),
                )

    def b_all_start(g):
        for p in range(3):
            _, b, _ = axes_of(g, p)
            arrived(c_recv[p].at[g, pl.ds(0, 3)], w_recv_sem.at[g, p, C_SUM])
            leaf = total_leaf(g, p)
            leaf[...] = c_recv[p][g, 0] + c_recv[p][g, 1] + c_recv[p][g, 2] + c_recv[p][g, 3]
            for d in range(1, 4):
                send(leaf, leaf, *sems(g, p, B_ALL), peer(b, lax.rem(at[b] + d, 4)))

    def a_all_start(g):
        for p in range(3):
            a, _, _ = axes_of(g, p)
            arrived(b_recv[p].at[g], w_recv_sem.at[g, p, B_ALL])
            block = total_block(g, p)
            for d in range(1, 4):
                send(block, block, *sems(g, p, A_ALL), peer(a, lax.rem(at[a] + d, 4)))

    def core_all_start(g):
        for p in range(3):
            first, width = PARTS[p]
            arrived(a_recv[p].at[g], w_recv_sem.at[g, p, A_ALL])
            part = total.at[g, :, pl.ds(pl.multiple_of(core * HALF + first, 128), width)]
            send(part, part, *sems(g, p, CORE_ALL), (dp, y * 2 + 1 - core))

    def core_all_done(g):
        for p in range(3):
            arrived(w_recv.at[g, :, part_cols(p)], w_recv_sem.at[g, p, CORE_ALL])

    member = lax.rem(dp, 8)
    mine = pl.ds(pl.multiple_of(8 * member, 8), 8)

    def gram_start():
        for g in range(2):
            g_part[:, g * RANK : (g + 1) * RANK] = nt(left[g], left[g], HP)
        for d in range(1, TENSOR):
            send(
                g_part.at[mine, :], g_recv.at[t],
                g_send_sem.at[0], g_recv_sem.at[0], (dp, lax.rem(t + d, TENSOR)),
            )
        g_recv[t] = g_part[mine, :]

    def gram_all_start():
        arrived(g_recv.at[pl.ds(0, 7)], g_recv_sem.at[0])
        summed = g_recv[0]
        for i in range(1, TENSOR):
            summed = summed + g_recv[i]
        g_all[mine, :] = summed
        for d in range(1, 8):
            other = 8 * (dp // 8) + lax.rem(member + d, 8)
            send(
                g_all.at[mine, :], g_all.at[mine, :],
                g_send_sem.at[1], g_recv_sem.at[1], (other, t),
            )

    lane = lax.broadcasted_iota(jnp.int32, (RANK, 2 * RANK), 1)
    row = lax.broadcasted_iota(jnp.int32, (RANK, 2 * RANK), 0)
    lane_one = lax.broadcasted_iota(jnp.int32, (1, 2 * RANK), 1)

    def gram_done():
        arrived(g_recv.at[pl.ds(0, 7)], g_recv_sem.at[1])
        work[...] = g_all[...]
        low[...] = jnp.where(lax.rem(lane, RANK) == row, 1.0, 0.0).astype(F32)

    def halves(value, lanes, column):
        gate = jnp.sum(jnp.where(lanes == column, value, 0.0), axis=1, keepdims=True)
        up = jnp.sum(jnp.where(lanes == column + RANK, value, 0.0), axis=1, keepdims=True)
        return jnp.where(lanes < RANK, gate, up)

    def eliminate(first, last):
        def step(j, carry):
            value = work[...]
            pivot_row = work[pl.ds(j, 1), :]
            low_row = low[pl.ds(j, 1), :]
            scale = 1.0 / halves(pivot_row, lane_one, j)
            factor = jnp.where(row > j, halves(value, lane, j) * scale, 0.0)
            work[...] = value - factor * pivot_row
            low[...] = low[...] - factor * low_row
            return carry

        lax.fori_loop(first, last, step, 0)

    def inverse_done():
        value = work[...]
        on = lax.rem(lane, RANK) == row
        gate = jnp.sum(jnp.where(on & (lane < RANK), value, 0.0), axis=1, keepdims=True)
        up = jnp.sum(jnp.where(on & (lane >= RANK), value, 0.0), axis=1, keepdims=True)
        diagonal = jnp.where(lane < RANK, gate, up)
        inverse[...] = low[...] / jnp.sqrt(diagonal)

    p_compute(0)
    pl.semaphore_wait(barrier, DP + TENSOR - 2)
    p_sum_start(0)
    p_compute(1)
    p_sum_start(1)
    p_all_start(0)
    p_all_start(1)
    p_done(0)
    core_start(0)
    a_start(0)
    p_done(1)
    gram_start()
    core_start(1)
    b_start(0)
    a_start(1)
    gram_all_start()
    c_start(0)
    b_start(1)
    gram_done()
    b_all_start(0)
    c_start(1)
    eliminate(0, 16)
    a_all_start(0)
    b_all_start(1)
    eliminate(16, 32)
    a_all_start(1)
    core_all_start(0)
    eliminate(32, RANK)
    inverse_done()
    core_all_start(1)
    core_all_done(0)
    core_all_done(1)

    for g in range(2):
        for phase in range(2):
            arrived(p_recv.at[g], p_send_sem.at[g, phase])
        for p in range(3):
            cols = part_cols(p)
            arrived(w_recv.at[g, :, cols], w_send_sem.at[g, p, CORE_SUM])
            arrived(w_recv.at[g, :, cols], w_send_sem.at[g, p, CORE_ALL])
            for stage in (A_SUM, A_ALL):
                arrived(a_recv[p].at[g], w_send_sem.at[g, p, stage])
            for stage in (B_SUM, C_SUM, B_ALL):
                arrived(b_recv[p].at[g], w_send_sem.at[g, p, stage])
    for phase in range(2):
        arrived(g_recv.at[pl.ds(0, 7)], g_send_sem.at[phase])


BLOCKS = 7
BLOCK = D // BLOCKS


def finish_kernel(
    data, total, left, inverse, new_err_gate, new_err_up, new_q_gate, new_q_up,
    err_stage, q_stage, low_stack, ortho_stack, sem,
):
    err_out = (new_err_gate, new_err_up)
    q_out = (new_q_gate, new_q_up)
    for g in range(2):
        low = inverse[:, g * RANK : (g + 1) * RANK]
        column = jnp.concatenate(three(low), axis=0)
        low_stack[g] = jnp.concatenate([column, column, column], axis=1)
        ortho = nn(low, left[g], HP).T
        first = ortho.astype(BF16).astype(F32)
        second = ortho - first
        ortho_stack[g] = jnp.concatenate([first, first, second, second], axis=1).astype(BF16)

    def copies(g, cols):
        return (
            pltpu.make_async_copy(err_stage.at[g, :, cols], err_out[g].at[:, cols], sem.at[g, 0]),
            pltpu.make_async_copy(q_stage.at[g, :, cols], q_out[g].at[:, cols], sem.at[g, 1]),
        )

    def step(i, carry):
        cols = pl.ds(pl.multiple_of(i * BLOCK, BLOCK), BLOCK)
        for g in range(2):
            summed = jnp.concatenate(three(total[g, :, cols]), axis=0)
            terms = nn(low_stack[g], summed)
            new_q = (terms[:RANK] + terms[RANK : 2 * RANK] + terms[2 * RANK :]) * (1.0 / DP)
            q_stage[g, :, cols] = new_q
            first = new_q.astype(BF16)
            second = (new_q - first.astype(F32)).astype(BF16)
            approx = nn(
                ortho_stack[g], jnp.concatenate([first, second, first, second], axis=0)
            )
            grad = data[pl.ds(2 * g * ROWS, ROWS), cols].astype(F32)
            err = data[pl.ds((2 * g + 1) * ROWS, ROWS), cols].astype(F32)
            err_stage[g, :, cols] = (grad + err - approx).astype(BF16)
            for copy in copies(g, cols):
                copy.start()
        return carry

    lax.fori_loop(0, BLOCKS, step, 0)
    for g in range(2):
        for copy in copies(g, pl.ds(0, D)):
            copy.wait()


def body(grad_gate, grad_up, err_gate, err_up, q_gate, q_up):
    def part_scratch(*lead):
        def of(divide, rows):
            return [pltpu.VMEM(lead + (rows, width // divide), F32) for _, width in PARTS]

        return of

    data, total, left, inverse = pl.pallas_call(
        exchange_kernel,
        out_shape=(
            pltpu.VMEM((4 * ROWS, D), BF16),
            pltpu.VMEM((2, RANK, D), F32),
            pltpu.VMEM((2, RANK, ROWS), F32),
            pltpu.VMEM((RANK, 2 * RANK), F32),
        ),
        in_specs=[pl.BlockSpec(memory_space=pl.ANY)] * 6,
        out_specs=[pl.BlockSpec(memory_space=pltpu.VMEM)] * 4,
        scratch_shapes=[
            pltpu.VMEM((2, RANK, D), F32),
            pltpu.VMEM((2 * ROWS, 3 * RANK), F32),
            pltpu.VMEM((2, RANK, ROWS), F32),
            pltpu.VMEM((2, DP - 1, 8, 128), F32),
            pltpu.VMEM((2, 3 * RANK, 2 * ROWS), BF16),
            pltpu.VMEM((2, RANK, HALF), F32),
            pltpu.VMEM((2, RANK, HALF), F32),
            pltpu.VMEM((2, RANK, HALF), F32),
            *part_scratch(2, 3)(1, 16),
            *part_scratch(2)(1, 16),
            *part_scratch(2, 3)(2, 8),
            *part_scratch(2, 4)(2, 8),
            pltpu.VMEM((RANK, 2 * RANK), F32),
            pltpu.VMEM((TENSOR, 8, 2 * RANK), F32),
            pltpu.VMEM((RANK, 2 * RANK), F32),
            pltpu.VMEM((RANK, 2 * RANK), F32),
            pltpu.VMEM((RANK, 2 * RANK), F32),
            pltpu.SemaphoreType.DMA((2, CHUNKS, 3)),
            pltpu.SemaphoreType.DMA((2, 2)),
            pltpu.SemaphoreType.DMA((2, 2)),
            pltpu.SemaphoreType.DMA((2,)),
            pltpu.SemaphoreType.DMA((2,)),
            pltpu.SemaphoreType.DMA((2, 3, STAGES)),
            pltpu.SemaphoreType.DMA((2, 3, STAGES)),
        ],
        compiler_params=pltpu.CompilerParams(
            collective_id=0, has_side_effects=True, vmem_limit_bytes=20 * 2**20
        ),
        name="exchange",
    )(
        *(
            pltpu.with_memory_space_constraint(v, pltpu.HBM)
            for v in (
                grad_gate.reshape(ROWS, D), err_gate.reshape(ROWS, D),
                grad_up.reshape(ROWS, D), err_up.reshape(ROWS, D), q_gate.T, q_up.T,
            )
        )
    )
    held = [pltpu.with_memory_space_constraint(v, pltpu.VMEM) for v in (data, total, left, inverse)]
    new_err_gate, new_err_up, new_q_gate, new_q_up = pl.pallas_call(
        finish_kernel,
        out_shape=(
            jax.ShapeDtypeStruct((ROWS, D), BF16),
            jax.ShapeDtypeStruct((ROWS, D), BF16),
            jax.ShapeDtypeStruct((RANK, D), F32),
            jax.ShapeDtypeStruct((RANK, D), F32),
        ),
        in_specs=[pl.BlockSpec(memory_space=pltpu.VMEM)] * 4,
        out_specs=[pl.BlockSpec(memory_space=pl.ANY)] * 4,
        scratch_shapes=[
            pltpu.VMEM((2, ROWS, D), BF16),
            pltpu.VMEM((2, RANK, D), F32),
            pltpu.VMEM((2, 3 * RANK, 3 * RANK), BF16),
            pltpu.VMEM((2, ROWS, 4 * RANK), BF16),
            pltpu.SemaphoreType.DMA((2, 2)),
        ],
        compiler_params=pltpu.CompilerParams(vmem_limit_bytes=16 * 2**20),
        name="finish",
    )(*held)
    return (
        new_err_gate.reshape(1, ROWS, D),
        new_err_up.reshape(1, ROWS, D),
        new_q_gate.T,
        new_q_up.T,
    )


def solution(mesh):
    placed = P("dp", "tensor", None)
    return jax.shard_map(
        body,
        mesh=mesh,
        in_specs=(placed, placed, placed, placed, P(), P()),
        out_specs=(placed, placed, P(), P()),
        check_vma=False,
    )
```

time: 361 us -> 69.7 us (0.19)
  waiting for transfers between devices: 237 us -> 0 us
  Pallas kernels: 0 us -> 69 us
  matrix products: 55.3 us -> 0 us
  other arithmetic: 29 us -> 0 us
  blocking collectives: 23.4 us -> 0 us
  between operations: 14.2 us -> 0.64 us
    psum x2 -> x0, waiting for transfers between devices: 237 us -> none  [the longest x1 153 us: body(): summed_gate, summed_up = lax.psum((local_gate, local_up), ('dp', 'tensor'))]
    pallas_call x0 -> x2, Pallas kernels: none -> 69 us  [the longest x1 61.4 us: body(): pl.pallas_call(exchange_kernel, out_shape=(pltpu.VMEM((4 * ROWS, D), BF16...]
    dot_general x8 -> x0, matrix products: 53.1 us -> none  [the longest x1 10.1 us: body(): jnp.dot(mat_gate, q_gate, precision=hp, preferred_element_type=jnp.float32)]
    another operation x10 -> x0, other arithmetic: 24.1 us -> none  [the longest x6 13 us: orthonormal(): lower = jnp.linalg.cholesky(gram)]
    psum x1 -> x0, blocking collectives: 23.4 us -> none  [body(): lax.psum((gram_of(left_gate), gram_of(left_up)), 'tensor')]
    div x3 -> x0, other arithmetic: 4.87 us -> none  [the longest x1 3.05 us: body(): new_q_up = summed_up / replicas]
  transfers between devices with their start and end apart: 2 -> 0, of which waited for: 2 -> 0; matrix products, arithmetic and copies ran while one was open for 0% -> 0% of each run, Pallas kernels for 0% -> 0%
where the time goes in v1:
time: 69.7 us; the launch traced here: 69.6 us
  Pallas kernels  69 us (99%)
    pallas_call x1, Pallas kernels, body(): pl.pallas_call(exchange_kernel, out_shape=(pltpu.VMEM((4 * ROWS, D), BF16...  61.4 us
    pallas_call x1, Pallas kernels, body(): pl.pallas_call(finish_kernel, out_shape=(jax.ShapeDtypeStruct((ROWS, D),...  7.54 us

profile of v1, /device:TPU:1, one launch (start us, length us, event | category | flops | bytes accessed | tf_op | source)
XLA Modules:
  0.0 69.6 jit_solution(9365747336879069968)
XLA Ops:
  0.6 61.4 %exchange.1 = (bf16[1024,7168]{1,0:T(8,128)(2,1)S(1)}, f32[2,64,7168]{2,1,0:T(8,128)S(1)}, f32[2,64,256]{2,1,0:T(8,128)S(1)}, f32[64,128]{1,0:T(8,128)S(1)}) custom-call(bf16[256,7168]{1,0:T(8,128)(2,1)} %bitcast.10, bf16[256,7168]{1,0:T(8,128)(2,1)} %bitcast.11, bf16[256,7168]{1,0:T(8,128)(2,1)} %bitcast.12, bf16[256,7168]{1,0:T(8,128)(2,1)} %bitcast.13, ...), custom_call_target="tpu_custom_call" | custom-call | tf_op jit(solution)/shard_map/exchange/pallas_call | solution.py:449
  62.1 7.5 %finish.1 = (bf16[256,7168]{1,0:T(8,128)(2,1)}, bf16[256,7168]{1,0:T(8,128)(2,1)}, f32[64,7168]{1,0:T(8,128)}, f32[64,7168]{1,0:T(8,128)}) custom-call(bf16[1024,7168]{1,0:T(8,128)(2,1)S(1)} %get-tuple-element.12.data, f32[2,64,7168]{2,1,0:T(8,128)S(1)} %get-tuple-element.13.total, f32[2,64,256]{2,1,0:T(8,128)S(1)} %get-tuple-element.14.left, ...), custom_call_target="tpu_custom_call" | custom-call | tf_op jit(solution)/shard_map/finish/pallas_call | solution.py:499

commit v2 on v1

--- a/solution.py
+++ b/solution.py
@@ -22,6 +22,8 @@
 CHUNK = D // CHUNKS
 TILE = 256
 PARTS = ((0, 1280), (1280, 1280), (2560, 1024))
+BLOCKS = 4
+BLOCK = D // BLOCKS
 STAGES = 7
 CORE_SUM, A_SUM, B_SUM, C_SUM, B_ALL, A_ALL, CORE_ALL = range(STAGES)
 
@@ -44,15 +46,40 @@
     return jnp.dot(left, right, precision=precision, preferred_element_type=F32)
 
 
+def finish_stacks(low, left, low_stack, ortho_stack):
+    column = jnp.concatenate(three(low), axis=0)
+    low_stack[...] = jnp.concatenate([column, column, column], axis=1)
+    ortho = nn(low, left, HP).T
+    first = ortho.astype(BF16).astype(F32)
+    second = ortho - first
+    ortho_stack[...] = jnp.concatenate([first, first, second, second], axis=1).astype(BF16)
+
+
+def finish_block(cols, data, total, low_stack, ortho_stack, err_out, q_out):
+    summed = jnp.concatenate(three(total[:, cols]), axis=0)
+    terms = nn(low_stack[...], summed)
+    new_q = (terms[:RANK] + terms[RANK : 2 * RANK] + terms[2 * RANK :]) * (1.0 / DP)
+    q_out[:, cols] = new_q
+    first = new_q.astype(BF16)
+    second = (new_q - first.astype(F32)).astype(BF16)
+    approx = nn(ortho_stack[...], jnp.concatenate([first, second, first, second], axis=0))
+    grad = data[:ROWS, cols].astype(F32)
+    err = data[ROWS:, cols].astype(F32)
+    err_out[:, cols] = (grad + err - approx).astype(BF16)
+
+
 def exchange_kernel(
     grad_gate, err_gate, grad_up, err_up, q_gate, q_up,
-    data, total, left, inverse,
-    q_buf, p_acc, p_part, p_recv, p_stack, w_send, w_own, w_recv,
+    err_gate_out, q_gate_out, data_up, total_up, left, inverse,
+    data_gate, total_gate, low_stack, ortho_stack,
+    q_buf, p_acc, p_recv, p_stack, w_send, w_own, w_recv,
     a_recv0, a_recv1, a_recv2, a_sum0, a_sum1, a_sum2,
     b_recv0, b_recv1, b_recv2, c_recv0, c_recv1, c_recv2,
     g_part, g_recv, g_all, work, low,
     load_sem, p_send_sem, p_recv_sem, g_send_sem, g_recv_sem, w_send_sem, w_recv_sem,
 ):
+    data = (data_gate, data_up)
+    total = (total_gate, total_up)
     a_recv = (a_recv0, a_recv1, a_recv2)
     a_sum = (a_sum0, a_sum1, a_sum2)
     b_recv = (b_recv0, b_recv1, b_recv2)
@@ -62,6 +89,10 @@
     z, x = dp // 4, lax.rem(dp, 4)
     y, core = t // 2, lax.rem(t, 2)
     at = (x, y, z)
+    one = dp // DP + 1
+
+    def block(fn, *args):
+        lax.fori_loop(0, one, lambda i, carry: (fn(*args), carry)[1], 0)
 
     def peer(axis, v):
         px, py, pz = (v if axis == i else at[i] for i in range(3))
@@ -79,11 +110,11 @@
     sources = ((q_gate, grad_gate, err_gate), (q_up, grad_up, err_up))
 
     def load(g, c, k):
-        cols = pl.ds(c * CHUNK, CHUNK)
+        cols = pl.ds(pl.multiple_of(c * CHUNK, CHUNK), CHUNK)
         if k == 0:
             dst = q_buf.at[g, :, cols]
         else:
-            dst = data.at[pl.ds((2 * g + k - 1) * ROWS, ROWS), cols]
+            dst = data[g].at[pl.ds((k - 1) * ROWS, ROWS), cols]
         return pltpu.make_async_copy(sources[g][k].at[:, cols], dst, load_sem.at[g, c, k])
 
     for g in range(2):
@@ -101,49 +132,52 @@
             barrier, inc=1, device_id=(dp, lax.rem(t + d, TENSOR)), device_id_type=MESH
         )
 
-    def chunk_of(member):
-        return pl.ds(pl.multiple_of(8 * (member // 2), 8), 8), pl.ds(
-            pl.multiple_of(128 * lax.rem(member, 2), 128), 128
-        )
-
     def p_compute(g):
-        for c in range(CHUNKS):
+        p_acc[...] = jnp.zeros_like(p_acc)
+
+        def step(c, carry):
             for k in range(3):
                 load(g, c, k).wait()
-            q3 = jnp.concatenate(three(q_buf[g, :, c * CHUNK : (c + 1) * CHUNK]), axis=0)
-            both = nt(data[2 * g * ROWS : (2 * g + 2) * ROWS, c * CHUNK : (c + 1) * CHUNK], q3)
-            if c == 0:
-                p_acc[...] = both
-            else:
-                p_acc[...] += both
+            cols = pl.ds(pl.multiple_of(c * CHUNK, CHUNK), CHUNK)
+            q3 = jnp.concatenate(three(q_buf[g, :, cols]), axis=0)
+            p_acc[...] += nt(data[g][:, cols], q3)
+            return carry
+
+        lax.fori_loop(0, CHUNKS, step, 0)
         both = p_acc[:ROWS, :] + p_acc[ROWS:, :]
         turned = both.T
-        p_part[g] = turned[:RANK] + turned[RANK : 2 * RANK] + turned[2 * RANK :]
-
-    def p_sum_start(g):
-        for d in range(1, DP):
-            member = lax.rem(dp + d, DP)
-            rows, cols = chunk_of(member)
-            send(
-                p_part.at[g, rows, cols], p_recv.at[g, d - 1],
-                p_send_sem.at[g, 0], p_recv_sem.at[g, 0], (member, t),
-            )
-
-    def p_all_start(g):
-        arrived(p_recv.at[g], p_recv_sem.at[g, 0])
-        rows, cols = chunk_of(dp)
-        summed = p_part[g, rows, cols]
-        for d in range(DP - 1):
-            summed = summed + p_recv[g, d]
-        left[g, rows, cols] = summed
-        for d in range(1, DP):
-            send(
-                left.at[g, rows, cols], left.at[g, rows, cols],
-                p_send_sem.at[g, 1], p_recv_sem.at[g, 1], (lax.rem(dp + d, DP), t),
-            )
+        summed = turned[:RANK] + turned[RANK : 2 * RANK] + turned[2 * RANK :]
+        p_recv[g, 0, 0, x] = summed[: RANK // 2]
+        p_recv[g, 0, 1, z] = summed[RANK // 2 :]
+
+    def p_axis(step, h):
+        return 0 if step == h else 2
+
+    def p_start(g, step):
+        for h in range(2):
+            axis = p_axis(step, h)
+            mine = p_recv.at[g, step, h, at[axis]]
+            for d in range(1, 4):
+                send(
+                    mine, mine, p_send_sem.at[g, step, h], p_recv_sem.at[g, step, h],
+                    peer(axis, lax.rem(at[axis] + d, 4)),
+                )
+
+    def p_sum(g, step, h):
+        arrived(p_recv.at[g, step, h, pl.ds(0, 3)], p_recv_sem.at[g, step, h])
+        return (
+            p_recv[g, step, h, 0] + p_recv[g, step, h, 1]
+            + p_recv[g, step, h, 2] + p_recv[g, step, h, 3]
+        )
+
+    def p_turn(g):
+        for h in range(2):
+            p_recv[g, 1, h, at[p_axis(1, h)]] = p_sum(g, 0, h)
+        p_start(g, 1)
 
     def p_done(g):
-        arrived(p_recv.at[g], p_recv_sem.at[g, 1])
+        for h in range(2):
+            left[g, h * (RANK // 2) : (h + 1) * (RANK // 2)] = p_sum(g, 1, h)
         p3 = jnp.concatenate(three(left[g]), axis=0)
         p_stack[g, :, :ROWS] = p3
         p_stack[g, :, ROWS:] = p3
@@ -152,16 +186,12 @@
         first, width = PARTS[p]
         start = pl.multiple_of(half * HALF + first, 128)
 
-        def step(i, carry):
-            offset = pl.multiple_of(i * TILE, TILE)
-            cols = pl.ds(pl.multiple_of(start + offset, 128), TILE)
-            prod = nn(p_stack[g], data[pl.ds(2 * g * ROWS, 2 * ROWS), cols])
-            dst[g, :, pl.ds(pl.multiple_of(first + offset, 128), TILE)] = (
+        for i in range(width // TILE):
+            cols = pl.ds(pl.multiple_of(start + i * TILE, 128), TILE)
+            prod = nn(p_stack[g], data[g][:, cols])
+            dst[g, :, first + i * TILE : first + (i + 1) * TILE] = (
                 prod[:RANK] + prod[RANK : 2 * RANK] + prod[2 * RANK :]
             )
-            return carry
-
-        lax.fori_loop(0, width // TILE, step, 0)
 
     def sems(g, p, stage):
         return w_send_sem.at[g, p, stage], w_recv_sem.at[g, p, stage]
@@ -176,8 +206,7 @@
     def total_block(g, p):
         a, _, _ = axes_of(g, p)
         first, width = PARTS[p]
-        return total.at[
-            g,
+        return total[g].at[
             pl.ds(pl.multiple_of(16 * at[a], 16), 16),
             pl.ds(pl.multiple_of(core * HALF + first, 128), width),
         ]
@@ -187,8 +216,8 @@
         first, width = PARTS[p]
         row = 16 * at[a] + 8 * (at[b] // 2)
         col = core * HALF + first + (width // 2) * lax.rem(at[b], 2)
-        return total.at[
-            g, pl.ds(pl.multiple_of(row, 8), 8), pl.ds(pl.multiple_of(col, 128), width // 2)
+        return total[g].at[
+            pl.ds(pl.multiple_of(row, 8), 8), pl.ds(pl.multiple_of(col, 128), width // 2)
         ]
 
     def core_start(g):
@@ -199,10 +228,12 @@
                 *sems(g, p, CORE_SUM), (dp, y * 2 + 1 - core),
             )
 
+    def w_rest(g):
+        for p in range(3):
+            w_block(g, w_own, core, p)
+
     def a_start(g):
-        for p in range(3):
-            w_block(g, w_own, core, p)
-            first, width = PARTS[p]
+        def step(p):
             cols = part_cols(p)
             arrived(w_recv.at[g, :, cols], w_recv_sem.at[g, p, CORE_SUM])
             w_own[g, :, cols] += w_recv[g, :, cols]
@@ -215,8 +246,11 @@
                     *sems(g, p, A_SUM), peer(a, v),
                 )
 
+        for p in range(3):
+            block(step, p)
+
     def b_start(g):
-        for p in range(3):
+        def step(p):
             a, b, _ = axes_of(g, p)
             first, width = PARTS[p]
             arrived(a_recv[p].at[g], w_recv_sem.at[g, p, A_SUM])
@@ -231,6 +265,9 @@
                     *sems(g, p, B_SUM), peer(b, v),
                 )
 
+        for p in range(3):
+            block(step, p)
+
     def leaf_rows(v):
         return pl.ds(pl.multiple_of(8 * (v // 2), 8), 8)
 
@@ -238,7 +275,7 @@
         return pl.ds(pl.multiple_of((width // 2) * lax.rem(v, 2), 128), width // 2)
 
     def c_start(g):
-        for p in range(3):
+        def step(p):
             _, b, c = axes_of(g, p)
             first, width = PARTS[p]
             arrived(b_recv[p].at[g], w_recv_sem.at[g, p, B_SUM])
@@ -252,8 +289,11 @@
                     *sems(g, p, C_SUM), peer(c, lax.rem(at[c] + d, 4)),
                 )
 
+        for p in range(3):
+            block(step, p)
+
     def b_all_start(g):
-        for p in range(3):
+        def step(p):
             _, b, _ = axes_of(g, p)
             arrived(c_recv[p].at[g, pl.ds(0, 3)], w_recv_sem.at[g, p, C_SUM])
             leaf = total_leaf(g, p)
@@ -261,20 +301,29 @@
             for d in range(1, 4):
                 send(leaf, leaf, *sems(g, p, B_ALL), peer(b, lax.rem(at[b] + d, 4)))
 
+        for p in range(3):
+            block(step, p)
+
     def a_all_start(g):
-        for p in range(3):
+        def step(p):
             a, _, _ = axes_of(g, p)
             arrived(b_recv[p].at[g], w_recv_sem.at[g, p, B_ALL])
             block = total_block(g, p)
             for d in range(1, 4):
                 send(block, block, *sems(g, p, A_ALL), peer(a, lax.rem(at[a] + d, 4)))
 
+        for p in range(3):
+            block(step, p)
+
     def core_all_start(g):
-        for p in range(3):
+        def step(p):
             first, width = PARTS[p]
             arrived(a_recv[p].at[g], w_recv_sem.at[g, p, A_ALL])
-            part = total.at[g, :, pl.ds(pl.multiple_of(core * HALF + first, 128), width)]
+            part = total[g].at[:, pl.ds(pl.multiple_of(core * HALF + first, 128), width)]
             send(part, part, *sems(g, p, CORE_ALL), (dp, y * 2 + 1 - core))
+
+        for p in range(3):
+            block(step, p)
 
     def core_all_done(g):
         for p in range(3):
@@ -341,42 +390,55 @@
         diagonal = jnp.where(lane < RANK, gate, up)
         inverse[...] = low[...] / jnp.sqrt(diagonal)
 
+    def finish_gate():
+        finish_stacks(inverse[:, :RANK], left[0], low_stack, ortho_stack)
+        for i in range(BLOCKS):
+            finish_block(
+                slice(i * BLOCK, (i + 1) * BLOCK), data_gate, total_gate, low_stack, ortho_stack,
+                err_gate_out, q_gate_out,
+            )
+
     p_compute(0)
     pl.semaphore_wait(barrier, DP + TENSOR - 2)
-    p_sum_start(0)
+    p_start(0, 0)
     p_compute(1)
-    p_sum_start(1)
-    p_all_start(0)
-    p_all_start(1)
-    p_done(0)
-    core_start(0)
+    p_start(1, 0)
+    block(p_turn, 0)
+    block(p_turn, 1)
+    block(p_done, 0)
+    block(core_start, 0)
+    block(w_rest, 0)
     a_start(0)
-    p_done(1)
-    gram_start()
-    core_start(1)
+    block(p_done, 1)
+    block(core_start, 1)
+    block(gram_start)
+    block(w_rest, 1)
     b_start(0)
     a_start(1)
-    gram_all_start()
+    block(gram_all_start)
     c_start(0)
     b_start(1)
-    gram_done()
+    block(gram_done)
     b_all_start(0)
+    eliminate(0, 8)
     c_start(1)
-    eliminate(0, 16)
+    eliminate(8, 24)
     a_all_start(0)
     b_all_start(1)
-    eliminate(16, 32)
+    eliminate(24, 40)
     a_all_start(1)
+    eliminate(40, RANK)
+    block(inverse_done)
     core_all_start(0)
-    eliminate(32, RANK)
-    inverse_done()
+    core_all_done(0)
+    block(finish_gate)
     core_all_start(1)
-    core_all_done(0)
     core_all_done(1)
 
     for g in range(2):
-        for phase in range(2):
-            arrived(p_recv.at[g], p_send_sem.at[g, phase])
+        for step in range(2):
+            for h in range(2):
+                arrived(p_recv.at[g, step, h, pl.ds(0, 3)], p_send_sem.at[g, step, h])
         for p in range(3):
             cols = part_cols(p)
             arrived(w_recv.at[g, :, cols], w_send_sem.at[g, p, CORE_SUM])
@@ -389,54 +451,40 @@
         arrived(g_recv.at[pl.ds(0, 7)], g_send_sem.at[phase])
 
 
-BLOCKS = 7
-BLOCK = D // BLOCKS
-
-
 def finish_kernel(
-    data, total, left, inverse, new_err_gate, new_err_up, new_q_gate, new_q_up,
-    err_stage, q_stage, low_stack, ortho_stack, sem,
+    err_gate, q_gate, data, total, left, inverse,
+    new_err_gate, new_err_up, new_q_gate, new_q_up,
+    err_up, q_up, low_stack, ortho_stack, sem,
 ):
-    err_out = (new_err_gate, new_err_up)
-    q_out = (new_q_gate, new_q_up)
-    for g in range(2):
-        low = inverse[:, g * RANK : (g + 1) * RANK]
-        column = jnp.concatenate(three(low), axis=0)
-        low_stack[g] = jnp.concatenate([column, column, column], axis=1)
-        ortho = nn(low, left[g], HP).T
-        first = ortho.astype(BF16).astype(F32)
-        second = ortho - first
-        ortho_stack[g] = jnp.concatenate([first, first, second, second], axis=1).astype(BF16)
-
-    def copies(g, cols):
+    gate = (
+        pltpu.make_async_copy(err_gate, new_err_gate, sem.at[0]),
+        pltpu.make_async_copy(q_gate, new_q_gate, sem.at[1]),
+    )
+    for copy in gate:
+        copy.start()
+    finish_stacks(inverse[:, RANK:], left[1], low_stack, ortho_stack)
+
+    def copies(i):
+        cols = pl.ds(pl.multiple_of(i * BLOCK, BLOCK), BLOCK)
         return (
-            pltpu.make_async_copy(err_stage.at[g, :, cols], err_out[g].at[:, cols], sem.at[g, 0]),
-            pltpu.make_async_copy(q_stage.at[g, :, cols], q_out[g].at[:, cols], sem.at[g, 1]),
+            pltpu.make_async_copy(err_up.at[:, cols], new_err_up.at[:, cols], sem.at[2]),
+            pltpu.make_async_copy(q_up.at[:, cols], new_q_up.at[:, cols], sem.at[3]),
         )
 
     def step(i, carry):
-        cols = pl.ds(pl.multiple_of(i * BLOCK, BLOCK), BLOCK)
-        for g in range(2):
-            summed = jnp.concatenate(three(total[g, :, cols]), axis=0)
-            terms = nn(low_stack[g], summed)
-            new_q = (terms[:RANK] + terms[RANK : 2 * RANK] + terms[2 * RANK :]) * (1.0 / DP)
-            q_stage[g, :, cols] = new_q
-            first = new_q.astype(BF16)
-            second = (new_q - first.astype(F32)).astype(BF16)
-            approx = nn(
-                ortho_stack[g], jnp.concatenate([first, second, first, second], axis=0)
-            )
-            grad = data[pl.ds(2 * g * ROWS, ROWS), cols].astype(F32)
-            err = data[pl.ds((2 * g + 1) * ROWS, ROWS), cols].astype(F32)
-            err_stage[g, :, cols] = (grad + err - approx).astype(BF16)
-            for copy in copies(g, cols):
-                copy.start()
+        finish_block(
+            pl.ds(pl.multiple_of(i * BLOCK, BLOCK), BLOCK), data, total, low_stack, ortho_stack,
+            err_up, q_up,
+        )
+        for copy in copies(i):
+            copy.start()
         return carry
 
     lax.fori_loop(0, BLOCKS, step, 0)
-    for g in range(2):
-        for copy in copies(g, pl.ds(0, D)):
-            copy.wait()
+    for copy in gate:
+        copy.wait()
+    pltpu.make_async_copy(err_up, new_err_up, sem.at[2]).wait()
+    pltpu.make_async_copy(q_up, new_q_up, sem.at[3]).wait()
 
 
 def body(grad_gate, grad_up, err_gate, err_up, q_gate, q_up):
@@ -446,21 +494,26 @@
 
         return of
 
-    data, total, left, inverse = pl.pallas_call(
+    made = pl.pallas_call(
         exchange_kernel,
         out_shape=(
-            pltpu.VMEM((4 * ROWS, D), BF16),
-            pltpu.VMEM((2, RANK, D), F32),
+            pltpu.VMEM((ROWS, D), BF16),
+            pltpu.VMEM((RANK, D), F32),
+            pltpu.VMEM((2 * ROWS, D), BF16),
+            pltpu.VMEM((RANK, D), F32),
             pltpu.VMEM((2, RANK, ROWS), F32),
             pltpu.VMEM((RANK, 2 * RANK), F32),
         ),
         in_specs=[pl.BlockSpec(memory_space=pl.ANY)] * 6,
-        out_specs=[pl.BlockSpec(memory_space=pltpu.VMEM)] * 4,
+        out_specs=[pl.BlockSpec(memory_space=pltpu.VMEM)] * 6,
         scratch_shapes=[
+            pltpu.VMEM((2 * ROWS, D), BF16),
+            pltpu.VMEM((RANK, D), F32),
+            pltpu.VMEM((3 * RANK, 3 * RANK), BF16),
+            pltpu.VMEM((ROWS, 4 * RANK), BF16),
             pltpu.VMEM((2, RANK, D), F32),
             pltpu.VMEM((2 * ROWS, 3 * RANK), F32),
-            pltpu.VMEM((2, RANK, ROWS), F32),
-            pltpu.VMEM((2, DP - 1, 8, 128), F32),
+            pltpu.VMEM((2, 2, 2, 4, RANK // 2, ROWS), F32),
             pltpu.VMEM((2, 3 * RANK, 2 * ROWS), BF16),
             pltpu.VMEM((2, RANK, HALF), F32),
             pltpu.VMEM((2, RANK, HALF), F32),
@@ -475,15 +528,15 @@
             pltpu.VMEM((RANK, 2 * RANK), F32),
             pltpu.VMEM((RANK, 2 * RANK), F32),
             pltpu.SemaphoreType.DMA((2, CHUNKS, 3)),
-            pltpu.SemaphoreType.DMA((2, 2)),
-            pltpu.SemaphoreType.DMA((2, 2)),
+            pltpu.SemaphoreType.DMA((2, 2, 2)),
+            pltpu.SemaphoreType.DMA((2, 2, 2)),
             pltpu.SemaphoreType.DMA((2,)),
             pltpu.SemaphoreType.DMA((2,)),
             pltpu.SemaphoreType.DMA((2, 3, STAGES)),
             pltpu.SemaphoreType.DMA((2, 3, STAGES)),
         ],
         compiler_params=pltpu.CompilerParams(
-            collective_id=0, has_side_effects=True, vmem_limit_bytes=20 * 2**20
+            collective_id=0, has_side_effects=True, vmem_limit_bytes=32 * 2**20
         ),
         name="exchange",
     )(
@@ -495,7 +548,7 @@
             )
         )
     )
-    held = [pltpu.with_memory_space_constraint(v, pltpu.VMEM) for v in (data, total, left, inverse)]
+    held = [pltpu.with_memory_space_constraint(v, pltpu.VMEM) for v in made]
     new_err_gate, new_err_up, new_q_gate, new_q_up = pl.pallas_call(
         finish_kernel,
         out_shape=(
@@ -504,16 +557,16 @@
             jax.ShapeDtypeStruct((RANK, D), F32),
             jax.ShapeDtypeStruct((RANK, D), F32),
         ),
-        in_specs=[pl.BlockSpec(memory_space=pltpu.VMEM)] * 4,
+        in_specs=[pl.BlockSpec(memory_space=pltpu.VMEM)] * 6,
         out_specs=[pl.BlockSpec(memory_space=pl.ANY)] * 4,
         scratch_shapes=[
-            pltpu.VMEM((2, ROWS, D), BF16),
-            pltpu.VMEM((2, RANK, D), F32),
-            pltpu.VMEM((2, 3 * RANK, 3 * RANK), BF16),
-            pltpu.VMEM((2, ROWS, 4 * RANK), BF16),
-            pltpu.SemaphoreType.DMA((2, 2)),
+            pltpu.VMEM((ROWS, D), BF16),
+            pltpu.VMEM((RANK, D), F32),
+            pltpu.VMEM((3 * RANK, 3 * RANK), BF16),
+            pltpu.VMEM((ROWS, 4 * RANK), BF16),
+            pltpu.SemaphoreType.DMA((4,)),
         ],
-        compiler_params=pltpu.CompilerParams(vmem_limit_bytes=16 * 2**20),
+        compiler_params=pltpu.CompilerParams(vmem_limit_bytes=12 * 2**20),
         name="finish",
     )(*held)
     return (

time: 69.7 us -> 62.3 us (0.89)
  Pallas kernels: 69 us -> 61.5 us
    pallas_call x1, Pallas kernels: 61.4 us -> 57.4 us  [body(): pl.pallas_call(exchange_kernel, out_shape=(pltpu.VMEM((ROWS, D), BF16), p...]
    pallas_call x1, Pallas kernels: 7.54 us -> 4.13 us  [body(): pl.pallas_call(finish_kernel, out_shape=(jax.ShapeDtypeStruct((ROWS, D),...]
where the time goes in v2:
time: 62.3 us; the launch traced here: 62.2 us
  Pallas kernels  61.5 us (99%)
  between operations  0.64 us (1%)
    pallas_call x1, Pallas kernels, body(): pl.pallas_call(exchange_kernel, out_shape=(pltpu.VMEM((ROWS, D), BF16), p...  57.4 us
    pallas_call x1, Pallas kernels, body(): pl.pallas_call(finish_kernel, out_shape=(jax.ShapeDtypeStruct((ROWS, D),...  4.13 us

profile of v2, /device:TPU:1, one launch (start us, length us, event | category | flops | bytes accessed | tf_op | source)
XLA Modules:
  0.0 62.2 jit_solution(11401979693183709980)
XLA Ops:
  0.6 57.4 %exchange.1 = (bf16[256,7168]{1,0:T(8,128)(2,1)S(1)}, f32[64,7168]{1,0:T(8,128)S(1)}, bf16[512,7168]{1,0:T(8,128)(2,1)S(1)}, f32[64,7168]{1,0:T(8,128)S(1)}, f32...) custom-call(bf16[256,7168]{1,0:T(8,128)(2,1)} %bitcast.10, bf16[256,7168]{1,0:T(8,128)(2,1)} %bitcast.11, ...), custom_call_target="tpu_custom_call" | custom-call | tf_op jit(solution)/shard_map/exchange/pallas_call | solution.py:497
  58.0 4.1 %finish.1 = (bf16[256,7168]{1,0:T(8,128)(2,1)}, bf16[256,7168]{1,0:T(8,128)(2,1)}, f32[64,7168]{1,0:T(8,128)}, f32[64,7168]{1,0:T(8,128)}) custom-call(bf16[256,7168]{1,0:T(8,128)(2,1)S(1)} %get-tuple-element.14.err_gate, f32[64,7168]{1,0:T(8,128)S(1)} %get-tuple-element.15.q_gate, bf16[512,7168]{1,0:T(8,128)(2,1)S(1)} %get-tuple-element.16.data, ...), custom_call_target="tpu_custom_call" | custom-call | tf_op jit(solution)/shard_map/finish/pallas_call | solution.py:552

commit v3 on v2

--- a/solution.py
+++ b/solution.py
@@ -221,12 +221,15 @@
         ]
 
     def core_start(g):
-        for p in range(3):
+        def step(p):
             w_block(g, w_send, 1 - core, p)
             send(
                 w_send.at[g, :, part_cols(p)], w_recv.at[g, :, part_cols(p)],
                 *sems(g, p, CORE_SUM), (dp, y * 2 + 1 - core),
             )
+
+        for p in range(3):
+            block(step, p)
 
     def w_rest(g):
         for p in range(3):
@@ -406,33 +409,32 @@
     block(p_turn, 0)
     block(p_turn, 1)
     block(p_done, 0)
-    block(core_start, 0)
+    core_start(0)
     block(w_rest, 0)
     a_start(0)
     block(p_done, 1)
-    block(core_start, 1)
+    core_start(1)
+    block(w_rest, 1)
     block(gram_start)
-    block(w_rest, 1)
+    a_start(1)
     b_start(0)
-    a_start(1)
     block(gram_all_start)
+    b_start(1)
     c_start(0)
-    b_start(1)
     block(gram_done)
+    eliminate(0, 20)
+    c_start(1)
     b_all_start(0)
-    eliminate(0, 8)
-    c_start(1)
-    eliminate(8, 24)
+    eliminate(20, 42)
+    b_all_start(1)
     a_all_start(0)
-    b_all_start(1)
-    eliminate(24, 40)
+    eliminate(42, RANK)
+    block(inverse_done)
     a_all_start(1)
-    eliminate(40, RANK)
-    block(inverse_done)
     core_all_start(0)
+    core_all_start(1)
     core_all_done(0)
     block(finish_gate)
-    core_all_start(1)
     core_all_done(1)
 
     for g in range(2):

time: 62.3 us -> 57.4 us (0.921)
  Pallas kernels: 61.5 us -> 56.7 us
    pallas_call x1, Pallas kernels: 57.4 us -> 52.5 us  [body(): pl.pallas_call(exchange_kernel, out_shape=(pltpu.VMEM((ROWS, D), BF16), p...]
where the time goes in v3:
time: 57.4 us; the launch traced here: 57.3 us
  Pallas kernels  56.7 us (99%)
  between operations  0.64 us (1%)
    pallas_call x1, Pallas kernels, body(): pl.pallas_call(exchange_kernel, out_shape=(pltpu.VMEM((ROWS, D), BF16), p...  52.5 us
    pallas_call x1, Pallas kernels, body(): pl.pallas_call(finish_kernel, out_shape=(jax.ShapeDtypeStruct((ROWS, D),...  4.13 us

profile of v3, /device:TPU:1, one launch (start us, length us, event | category | flops | bytes accessed | tf_op | source)
XLA Modules:
  0.0 57.3 jit_solution(17537379754869742283)
XLA Ops:
  0.6 52.5 %exchange.1 = (bf16[256,7168]{1,0:T(8,128)(2,1)S(1)}, f32[64,7168]{1,0:T(8,128)S(1)}, bf16[512,7168]{1,0:T(8,128)(2,1)S(1)}, f32[64,7168]{1,0:T(8,128)S(1)}, f32...) custom-call(bf16[256,7168]{1,0:T(8,128)(2,1)} %bitcast.10, bf16[256,7168]{1,0:T(8,128)(2,1)} %bitcast.11, ...), custom_call_target="tpu_custom_call" | custom-call | tf_op jit(solution)/shard_map/exchange/pallas_call | solution.py:499
  53.2 4.1 %finish.1 = (bf16[256,7168]{1,0:T(8,128)(2,1)}, bf16[256,7168]{1,0:T(8,128)(2,1)}, f32[64,7168]{1,0:T(8,128)}, f32[64,7168]{1,0:T(8,128)}) custom-call(bf16[256,7168]{1,0:T(8,128)(2,1)S(1)} %get-tuple-element.14.err_gate, f32[64,7168]{1,0:T(8,128)S(1)} %get-tuple-element.15.q_gate, bf16[512,7168]{1,0:T(8,128)(2,1)S(1)} %get-tuple-element.16.data, ...), custom_call_target="tpu_custom_call" | custom-call | tf_op jit(solution)/shard_map/finish/pallas_call | solution.py:554

commit v4 on v3

--- a/solution.py
+++ b/solution.py
@@ -24,8 +24,11 @@
 PARTS = ((0, 1280), (1280, 1280), (2560, 1024))
 BLOCKS = 4
 BLOCK = D // BLOCKS
-STAGES = 7
-CORE_SUM, A_SUM, B_SUM, C_SUM, B_ALL, A_ALL, CORE_ALL = range(STAGES)
+STAGES = 8
+CORE_SUM, A_SUM, B_SUM, C_SUM, B_ALL, A_ALL, CORE_ALL, A_FAR = range(STAGES)
+
+
+SUMS = (CORE_SUM, A_SUM, B_SUM, C_SUM, B_ALL)
 
 
 def three(value):
@@ -203,11 +206,10 @@
     def part_cols(p):
         return pl.ds(PARTS[p][0], PARTS[p][1])
 
-    def total_block(g, p):
-        a, _, _ = axes_of(g, p)
+    def total_block(g, p, v):
         first, width = PARTS[p]
         return total[g].at[
-            pl.ds(pl.multiple_of(16 * at[a], 16), 16),
+            pl.ds(pl.multiple_of(16 * v, 16), 16),
             pl.ds(pl.multiple_of(core * HALF + first, 128), width),
         ]
 
@@ -230,10 +232,6 @@
 
         for p in range(3):
             block(step, p)
-
-    def w_rest(g):
-        for p in range(3):
-            w_block(g, w_own, core, p)
 
     def a_start(g):
         def step(p):
@@ -250,6 +248,7 @@
                 )
 
         for p in range(3):
+            block(w_block, g, w_own, core, p)
             block(step, p)
 
     def b_start(g):
@@ -311,19 +310,28 @@
         def step(p):
             a, _, _ = axes_of(g, p)
             arrived(b_recv[p].at[g], w_recv_sem.at[g, p, B_ALL])
-            block = total_block(g, p)
-            for d in range(1, 4):
-                send(block, block, *sems(g, p, A_ALL), peer(a, lax.rem(at[a] + d, 4)))
+            mine = total_block(g, p, at[a])
+            for d in (1, 3, 2):
+                send(
+                    mine, mine, w_send_sem.at[g, p, A_ALL],
+                    w_recv_sem.at[g, p, A_FAR if d == 2 else A_ALL],
+                    peer(a, lax.rem(at[a] + d, 4)),
+                )
+            send(mine, mine, *sems(g, p, CORE_ALL), (dp, y * 2 + 1 - core))
 
         for p in range(3):
             block(step, p)
 
-    def core_all_start(g):
+    def core_all_start(g, far):
         def step(p):
-            first, width = PARTS[p]
-            arrived(a_recv[p].at[g], w_recv_sem.at[g, p, A_ALL])
-            part = total[g].at[:, pl.ds(pl.multiple_of(core * HALF + first, 128), width)]
-            send(part, part, *sems(g, p, CORE_ALL), (dp, y * 2 + 1 - core))
+            a, _, _ = axes_of(g, p)
+            if far:
+                arrived(a_recv[p].at[g, 0], w_recv_sem.at[g, p, A_FAR])
+            else:
+                arrived(a_recv[p].at[g, pl.ds(0, 2)], w_recv_sem.at[g, p, A_ALL])
+            for d in (2,) if far else (1, 3):
+                block_of = total_block(g, p, lax.rem(at[a] + d, 4))
+                send(block_of, block_of, *sems(g, p, CORE_ALL), (dp, y * 2 + 1 - core))
 
         for p in range(3):
             block(step, p)
@@ -401,6 +409,21 @@
                 err_gate_out, q_gate_out,
             )
 
+    def p_sent():
+        for g in range(2):
+            for step in range(2):
+                for h in range(2):
+                    arrived(p_recv.at[g, step, h, pl.ds(0, 3)], p_send_sem.at[g, step, h])
+        for phase in range(2):
+            arrived(g_recv.at[pl.ds(0, 7)], g_send_sem.at[phase])
+
+    def w_sent(g, stages):
+        for p in range(3):
+            half = w_recv.at[g, :, part_cols(p)]
+            refs = {CORE_SUM: half, CORE_ALL: half, A_SUM: a_recv[p].at[g], A_ALL: a_recv[p].at[g]}
+            for stage in stages:
+                arrived(refs.get(stage, b_recv[p].at[g]), w_send_sem.at[g, p, stage])
+
     p_compute(0)
     pl.semaphore_wait(barrier, DP + TENSOR - 2)
     p_start(0, 0)
@@ -410,13 +433,11 @@
     block(p_turn, 1)
     block(p_done, 0)
     core_start(0)
-    block(w_rest, 0)
     a_start(0)
     block(p_done, 1)
     core_start(1)
-    block(w_rest, 1)
+    a_start(1)
     block(gram_start)
-    a_start(1)
     b_start(0)
     block(gram_all_start)
     b_start(1)
@@ -428,29 +449,22 @@
     eliminate(20, 42)
     b_all_start(1)
     a_all_start(0)
-    eliminate(42, RANK)
+    eliminate(42, 50)
+    a_all_start(1)
+    eliminate(50, RANK)
     block(inverse_done)
-    a_all_start(1)
-    core_all_start(0)
-    core_all_start(1)
+    core_all_start(0, False)
+    core_all_start(0, True)
+    block(p_sent)
+    block(w_sent, 0, SUMS)
+    block(w_sent, 1, SUMS)
+    core_all_start(1, False)
     core_all_done(0)
     block(finish_gate)
+    block(w_sent, 0, (A_ALL, CORE_ALL))
+    core_all_start(1, True)
     core_all_done(1)
-
-    for g in range(2):
-        for step in range(2):
-            for h in range(2):
-                arrived(p_recv.at[g, step, h, pl.ds(0, 3)], p_send_sem.at[g, step, h])
-        for p in range(3):
-            cols = part_cols(p)
-            arrived(w_recv.at[g, :, cols], w_send_sem.at[g, p, CORE_SUM])
-            arrived(w_recv.at[g, :, cols], w_send_sem.at[g, p, CORE_ALL])
-            for stage in (A_SUM, A_ALL):
-                arrived(a_recv[p].at[g], w_send_sem.at[g, p, stage])
-            for stage in (B_SUM, C_SUM, B_ALL):
-                arrived(b_recv[p].at[g], w_send_sem.at[g, p, stage])
-    for phase in range(2):
-        arrived(g_recv.at[pl.ds(0, 7)], g_send_sem.at[phase])
+    block(w_sent, 1, (A_ALL, CORE_ALL))
 
 
 def finish_kernel(

time: 57.4 us -> 59.6 us (1.038)
  Pallas kernels: 56.7 us -> 58.9 us
    pallas_call x1, Pallas kernels: 52.5 us -> 54.7 us  [body(): pl.pallas_call(exchange_kernel, out_shape=(pltpu.VMEM((ROWS, D), BF16), p...]
where the time goes in v4:
time: 59.6 us; the launch traced here: 59.5 us
  Pallas kernels  58.9 us (99%)
  between operations  0.64 us (1%)
    pallas_call x1, Pallas kernels, body(): pl.pallas_call(exchange_kernel, out_shape=(pltpu.VMEM((ROWS, D), BF16), p...  54.7 us
    pallas_call x1, Pallas kernels, body(): pl.pallas_call(finish_kernel, out_shape=(jax.ShapeDtypeStruct((ROWS, D),...  4.13 us

profile of v4, /device:TPU:1, one launch (start us, length us, event | category | flops | bytes accessed | tf_op | source)
XLA Modules:
  0.0 59.5 jit_solution(7120814026677129467)
XLA Ops:
  0.6 54.7 %exchange.1 = (bf16[256,7168]{1,0:T(8,128)(2,1)S(1)}, f32[64,7168]{1,0:T(8,128)S(1)}, bf16[512,7168]{1,0:T(8,128)(2,1)S(1)}, f32[64,7168]{1,0:T(8,128)S(1)}, f32...) custom-call(bf16[256,7168]{1,0:T(8,128)(2,1)} %bitcast.10, bf16[256,7168]{1,0:T(8,128)(2,1)} %bitcast.11, ...), custom_call_target="tpu_custom_call" | custom-call | tf_op jit(solution)/shard_map/exchange/pallas_call | solution.py:513
  55.4 4.1 %finish.1 = (bf16[256,7168]{1,0:T(8,128)(2,1)}, bf16[256,7168]{1,0:T(8,128)(2,1)}, f32[64,7168]{1,0:T(8,128)}, f32[64,7168]{1,0:T(8,128)}) custom-call(bf16[256,7168]{1,0:T(8,128)(2,1)S(1)} %get-tuple-element.14.err_gate, f32[64,7168]{1,0:T(8,128)S(1)} %get-tuple-element.15.q_gate, bf16[512,7168]{1,0:T(8,128)(2,1)S(1)} %get-tuple-element.16.data, ...), custom_call_target="tpu_custom_call" | custom-call | tf_op jit(solution)/shard_map/finish/pallas_call | solution.py:568

commit v5 on v4

--- a/solution.py
+++ b/solution.py
@@ -18,10 +18,13 @@
 ROWS = 256
 RANK = 64
 HALF = D // 2
-CHUNKS = 4
-CHUNK = D // CHUNKS
+CHUNKS = ((0, 2048), (2048, 2048), (4096, 2048), (6144, 1024))
 TILE = 256
-PARTS = ((0, 1280), (1280, 1280), (2560, 1024))
+GROUPS = (
+    (0, ((0, 1280, 0), (1280, 1280, 1), (2560, 1024, 2))),
+    (1, ((0, 1280, 1), (1280, 1280, 2), (2560, 1024, 0))),
+)
+NG = len(GROUPS)
 BLOCKS = 4
 BLOCK = D // BLOCKS
 STAGES = 8
@@ -76,17 +79,16 @@
     err_gate_out, q_gate_out, data_up, total_up, left, inverse,
     data_gate, total_gate, low_stack, ortho_stack,
     q_buf, p_acc, p_recv, p_stack, w_send, w_own, w_recv,
-    a_recv0, a_recv1, a_recv2, a_sum0, a_sum1, a_sum2,
-    b_recv0, b_recv1, b_recv2, c_recv0, c_recv1, c_recv2,
     g_part, g_recv, g_all, work, low,
     load_sem, p_send_sem, p_recv_sem, g_send_sem, g_recv_sem, w_send_sem, w_recv_sem,
+    *part_refs,
 ):
     data = (data_gate, data_up)
     total = (total_gate, total_up)
-    a_recv = (a_recv0, a_recv1, a_recv2)
-    a_sum = (a_sum0, a_sum1, a_sum2)
-    b_recv = (b_recv0, b_recv1, b_recv2)
-    c_recv = (c_recv0, c_recv1, c_recv2)
+    a_recv, a_sum, b_recv, c_recv = (
+        [part_refs[(kind * NG + n) * 3 : (kind * NG + n) * 3 + 3] for n in range(NG)]
+        for kind in range(4)
+    )
     dp = lax.axis_index("dp")
     t = lax.axis_index("tensor")
     z, x = dp // 4, lax.rem(dp, 4)
@@ -113,7 +115,7 @@
     sources = ((q_gate, grad_gate, err_gate), (q_up, grad_up, err_up))
 
     def load(g, c, k):
-        cols = pl.ds(pl.multiple_of(c * CHUNK, CHUNK), CHUNK)
+        cols = pl.ds(*CHUNKS[c])
         if k == 0:
             dst = q_buf.at[g, :, cols]
         else:
@@ -121,7 +123,7 @@
         return pltpu.make_async_copy(sources[g][k].at[:, cols], dst, load_sem.at[g, c, k])
 
     for g in range(2):
-        for c in range(CHUNKS):
+        for c in range(len(CHUNKS)):
             for k in range(3):
                 load(g, c, k).start()
 
@@ -138,15 +140,15 @@
     def p_compute(g):
         p_acc[...] = jnp.zeros_like(p_acc)
 
-        def step(c, carry):
+        def step(c):
             for k in range(3):
                 load(g, c, k).wait()
-            cols = pl.ds(pl.multiple_of(c * CHUNK, CHUNK), CHUNK)
+            cols = pl.ds(*CHUNKS[c])
             q3 = jnp.concatenate(three(q_buf[g, :, cols]), axis=0)
             p_acc[...] += nt(data[g][:, cols], q3)
-            return carry
-
-        lax.fori_loop(0, CHUNKS, step, 0)
+
+        for c in range(len(CHUNKS)):
+            block(step, c)
         both = p_acc[:ROWS, :] + p_acc[ROWS:, :]
         turned = both.T
         summed = turned[:RANK] + turned[RANK : 2 * RANK] + turned[2 * RANK :]
@@ -160,7 +162,7 @@
         for h in range(2):
             axis = p_axis(step, h)
             mine = p_recv.at[g, step, h, at[axis]]
-            for d in range(1, 4):
+            for d in (2, 1, 3):
                 send(
                     mine, mine, p_send_sem.at[g, step, h], p_recv_sem.at[g, step, h],
                     peer(axis, lax.rem(at[axis] + d, 4)),
@@ -185,10 +187,10 @@
         p_stack[g, :, :ROWS] = p3
         p_stack[g, :, ROWS:] = p3
 
-    def w_block(g, dst, half, p):
-        first, width = PARTS[p]
+    def w_block(n, dst, half, p):
+        g, parts = GROUPS[n]
+        first, width, _ = parts[p]
         start = pl.multiple_of(half * HALF + first, 128)
-
         for i in range(width // TILE):
             cols = pl.ds(pl.multiple_of(start + i * TILE, 128), TILE)
             prod = nn(p_stack[g], data[g][:, cols])
@@ -196,149 +198,155 @@
                 prod[:RANK] + prod[RANK : 2 * RANK] + prod[2 * RANK :]
             )
 
-    def sems(g, p, stage):
-        return w_send_sem.at[g, p, stage], w_recv_sem.at[g, p, stage]
-
-    def axes_of(g, p):
-        first = (p + g) % 3
+    def sems(n, p, stage):
+        return w_send_sem.at[n, p, stage], w_recv_sem.at[n, p, stage]
+
+    def axes_of(n, p):
+        first = GROUPS[n][1][p][2]
         return first, (first + 1) % 3, (first + 2) % 3
 
-    def part_cols(p):
-        return pl.ds(PARTS[p][0], PARTS[p][1])
-
-    def total_block(g, p, v):
-        first, width = PARTS[p]
-        return total[g].at[
-            pl.ds(pl.multiple_of(16 * v, 16), 16),
-            pl.ds(pl.multiple_of(core * HALF + first, 128), width),
-        ]
-
-    def total_leaf(g, p):
-        a, b, _ = axes_of(g, p)
-        first, width = PARTS[p]
-        row = 16 * at[a] + 8 * (at[b] // 2)
-        col = core * HALF + first + (width // 2) * lax.rem(at[b], 2)
-        return total[g].at[
-            pl.ds(pl.multiple_of(row, 8), 8), pl.ds(pl.multiple_of(col, 128), width // 2)
-        ]
-
-    def core_start(g):
+    def half_part(ref, n, p):
+        g, parts = GROUPS[n]
+        first, width, _ = parts[p]
+        return ref.at[g, :, first : first + width]
+
+    def total_part(n, p, rows, skip, width):
+        g, parts = GROUPS[n]
+        col = pl.multiple_of(core * HALF + parts[p][0] + skip, 128)
+        return total[g].at[rows, pl.ds(col, width)]
+
+    def total_block(n, p, v):
+        rows = pl.ds(pl.multiple_of(16 * v, 16), 16)
+        return total_part(n, p, rows, 0, GROUPS[n][1][p][1])
+
+    def total_leaf(n, p):
+        a, b, _ = axes_of(n, p)
+        half = GROUPS[n][1][p][1] // 2
+        rows = pl.ds(pl.multiple_of(16 * at[a] + 8 * (at[b] // 2), 8), 8)
+        return total_part(n, p, rows, half * lax.rem(at[b], 2), half)
+
+    def leaf_rows(v):
+        return pl.ds(pl.multiple_of(8 * (v // 2), 8), 8)
+
+    def leaf_cols(n, p, v):
+        half = GROUPS[n][1][p][1] // 2
+        return pl.ds(pl.multiple_of(half * lax.rem(v, 2), 128), half)
+
+    other_core = (dp, y * 2 + 1 - core)
+
+    def core_start(n):
+        def other(p):
+            w_block(n, w_send, 1 - core, p)
+            send(
+                half_part(w_send, n, p), half_part(w_recv, n, p), *sems(n, p, CORE_SUM), other_core
+            )
+
+        def rest():
+            for p in range(3):
+                w_block(n, w_own, core, p)
+
+        for p in range(3):
+            block(other, p)
+        block(rest)
+
+    def a_start(n):
         def step(p):
-            w_block(g, w_send, 1 - core, p)
-            send(
-                w_send.at[g, :, part_cols(p)], w_recv.at[g, :, part_cols(p)],
-                *sems(g, p, CORE_SUM), (dp, y * 2 + 1 - core),
-            )
-
-        for p in range(3):
-            block(step, p)
-
-    def a_start(g):
-        def step(p):
-            cols = part_cols(p)
-            arrived(w_recv.at[g, :, cols], w_recv_sem.at[g, p, CORE_SUM])
-            w_own[g, :, cols] += w_recv[g, :, cols]
-            a, _, _ = axes_of(g, p)
-            for d in range(1, 4):
+            a, _, _ = axes_of(n, p)
+            mine, theirs = half_part(w_own, n, p), half_part(w_recv, n, p)
+            arrived(theirs, w_recv_sem.at[n, p, CORE_SUM])
+            mine[...] += theirs[...]
+            for d in (2, 1, 3):
                 v = lax.rem(at[a] + d, 4)
                 send(
-                    w_own.at[g, pl.ds(pl.multiple_of(16 * v, 16), 16), cols],
-                    a_recv[p].at[g, d - 1],
-                    *sems(g, p, A_SUM), peer(a, v),
+                    mine.at[pl.ds(pl.multiple_of(16 * v, 16), 16)], a_recv[n][p].at[d - 1],
+                    *sems(n, p, A_SUM), peer(a, v),
                 )
 
         for p in range(3):
-            block(w_block, g, w_own, core, p)
             block(step, p)
 
-    def b_start(g):
+    def b_start(n):
         def step(p):
-            a, b, _ = axes_of(g, p)
-            first, width = PARTS[p]
-            arrived(a_recv[p].at[g], w_recv_sem.at[g, p, A_SUM])
-            a_sum[p][g] = (
-                w_own[g, pl.ds(pl.multiple_of(16 * at[a], 16), 16), part_cols(p)]
-                + a_recv[p][g, 0] + a_recv[p][g, 1] + a_recv[p][g, 2]
-            )
-            for d in range(1, 4):
+            a, b, _ = axes_of(n, p)
+            arrived(a_recv[n][p], w_recv_sem.at[n, p, A_SUM])
+            mine = half_part(w_own, n, p).at[pl.ds(pl.multiple_of(16 * at[a], 16), 16)]
+            a_sum[n][p][...] = mine[...] + a_recv[n][p][0] + a_recv[n][p][1] + a_recv[n][p][2]
+            for d in (2, 1, 3):
                 v = lax.rem(at[b] + d, 4)
                 send(
-                    a_sum[p].at[g, leaf_rows(v), leaf_cols(v, width)], b_recv[p].at[g, d - 1],
-                    *sems(g, p, B_SUM), peer(b, v),
+                    a_sum[n][p].at[leaf_rows(v), leaf_cols(n, p, v)], b_recv[n][p].at[d - 1],
+                    *sems(n, p, B_SUM), peer(b, v),
                 )
 
         for p in range(3):
             block(step, p)
 
-    def leaf_rows(v):
-        return pl.ds(pl.multiple_of(8 * (v // 2), 8), 8)
-
-    def leaf_cols(v, width):
-        return pl.ds(pl.multiple_of((width // 2) * lax.rem(v, 2), 128), width // 2)
-
-    def c_start(g):
+    def c_start(n):
         def step(p):
-            _, b, c = axes_of(g, p)
-            first, width = PARTS[p]
-            arrived(b_recv[p].at[g], w_recv_sem.at[g, p, B_SUM])
-            c_recv[p][g, at[c]] = (
-                a_sum[p][g, leaf_rows(at[b]), leaf_cols(at[b], width)]
-                + b_recv[p][g, 0] + b_recv[p][g, 1] + b_recv[p][g, 2]
+            _, b, c = axes_of(n, p)
+            arrived(b_recv[n][p], w_recv_sem.at[n, p, B_SUM])
+            c_recv[n][p][at[c]] = (
+                a_sum[n][p][leaf_rows(at[b]), leaf_cols(n, p, at[b])]
+                + b_recv[n][p][0] + b_recv[n][p][1] + b_recv[n][p][2]
             )
-            for d in range(1, 4):
+            mine = c_recv[n][p].at[at[c]]
+            for d in (2, 1, 3):
+                send(mine, mine, *sems(n, p, C_SUM), peer(c, lax.rem(at[c] + d, 4)))
+
+        for p in range(3):
+            block(step, p)
+
+    def b_all_start(n):
+        def step(p):
+            _, b, _ = axes_of(n, p)
+            arrived(c_recv[n][p].at[pl.ds(0, 3)], w_recv_sem.at[n, p, C_SUM])
+            leaf = total_leaf(n, p)
+            parts = c_recv[n][p]
+            leaf[...] = parts[0] + parts[1] + parts[2] + parts[3]
+            for d in (2, 1, 3):
+                send(leaf, leaf, *sems(n, p, B_ALL), peer(b, lax.rem(at[b] + d, 4)))
+
+        for p in range(3):
+            block(step, p)
+
+    def a_all_start(n):
+        def step(p):
+            a, _, _ = axes_of(n, p)
+            arrived(b_recv[n][p], w_recv_sem.at[n, p, B_ALL])
+            mine = total_block(n, p, at[a])
+            for d in (2, 1, 3):
                 send(
-                    c_recv[p].at[g, at[c]], c_recv[p].at[g, at[c]],
-                    *sems(g, p, C_SUM), peer(c, lax.rem(at[c] + d, 4)),
-                )
-
-        for p in range(3):
-            block(step, p)
-
-    def b_all_start(g):
-        def step(p):
-            _, b, _ = axes_of(g, p)
-            arrived(c_recv[p].at[g, pl.ds(0, 3)], w_recv_sem.at[g, p, C_SUM])
-            leaf = total_leaf(g, p)
-            leaf[...] = c_recv[p][g, 0] + c_recv[p][g, 1] + c_recv[p][g, 2] + c_recv[p][g, 3]
-            for d in range(1, 4):
-                send(leaf, leaf, *sems(g, p, B_ALL), peer(b, lax.rem(at[b] + d, 4)))
-
-        for p in range(3):
-            block(step, p)
-
-    def a_all_start(g):
-        def step(p):
-            a, _, _ = axes_of(g, p)
-            arrived(b_recv[p].at[g], w_recv_sem.at[g, p, B_ALL])
-            mine = total_block(g, p, at[a])
-            for d in (1, 3, 2):
-                send(
-                    mine, mine, w_send_sem.at[g, p, A_ALL],
-                    w_recv_sem.at[g, p, A_FAR if d == 2 else A_ALL],
+                    mine, mine, w_send_sem.at[n, p, A_ALL],
+                    w_recv_sem.at[n, p, A_FAR if d == 2 else A_ALL],
                     peer(a, lax.rem(at[a] + d, 4)),
                 )
-            send(mine, mine, *sems(g, p, CORE_ALL), (dp, y * 2 + 1 - core))
+            send(mine, mine, *sems(n, p, CORE_ALL), other_core)
 
         for p in range(3):
             block(step, p)
 
-    def core_all_start(g, far):
-        def step(p):
-            a, _, _ = axes_of(g, p)
-            if far:
-                arrived(a_recv[p].at[g, 0], w_recv_sem.at[g, p, A_FAR])
-            else:
-                arrived(a_recv[p].at[g, pl.ds(0, 2)], w_recv_sem.at[g, p, A_ALL])
-            for d in (2,) if far else (1, 3):
-                block_of = total_block(g, p, lax.rem(at[a] + d, 4))
-                send(block_of, block_of, *sems(g, p, CORE_ALL), (dp, y * 2 + 1 - core))
-
-        for p in range(3):
-            block(step, p)
-
-    def core_all_done(g):
-        for p in range(3):
-            arrived(w_recv.at[g, :, part_cols(p)], w_recv_sem.at[g, p, CORE_ALL])
+    def core_all_start(n):
+        def far(p):
+            a, _, _ = axes_of(n, p)
+            arrived(a_recv[n][p].at[0], w_recv_sem.at[n, p, A_FAR])
+            there = total_block(n, p, lax.rem(at[a] + 2, 4))
+            send(there, there, *sems(n, p, CORE_ALL), other_core)
+
+        def near(p):
+            a, _, _ = axes_of(n, p)
+            arrived(a_recv[n][p].at[pl.ds(0, 2)], w_recv_sem.at[n, p, A_ALL])
+            for d in (1, 3):
+                there = total_block(n, p, lax.rem(at[a] + d, 4))
+                send(there, there, *sems(n, p, CORE_ALL), other_core)
+
+        for p in range(3):
+            block(far, p)
+        for p in range(3):
+            block(near, p)
+
+    def core_all_done(n):
+        for p in range(3):
+            arrived(half_part(w_recv, n, p), w_recv_sem.at[n, p, CORE_ALL])
 
     member = lax.rem(dp, 8)
     mine = pl.ds(pl.multiple_of(8 * member, 8), 8)
@@ -417,12 +425,12 @@
         for phase in range(2):
             arrived(g_recv.at[pl.ds(0, 7)], g_send_sem.at[phase])
 
-    def w_sent(g, stages):
-        for p in range(3):
-            half = w_recv.at[g, :, part_cols(p)]
-            refs = {CORE_SUM: half, CORE_ALL: half, A_SUM: a_recv[p].at[g], A_ALL: a_recv[p].at[g]}
+    def w_sent(n, stages):
+        for p in range(3):
+            half = half_part(w_recv, n, p)
+            refs = {CORE_SUM: half, CORE_ALL: half, A_SUM: a_recv[n][p], A_ALL: a_recv[n][p]}
             for stage in stages:
-                arrived(refs.get(stage, b_recv[p].at[g]), w_send_sem.at[g, p, stage])
+                arrived(refs.get(stage, b_recv[n][p]), w_send_sem.at[n, p, stage])
 
     p_compute(0)
     pl.semaphore_wait(barrier, DP + TENSOR - 2)
@@ -436,35 +444,33 @@
     a_start(0)
     block(p_done, 1)
     core_start(1)
+    block(gram_start)
     a_start(1)
-    block(gram_start)
     b_start(0)
     block(gram_all_start)
     b_start(1)
     c_start(0)
     block(gram_done)
-    eliminate(0, 20)
+    eliminate(0, 16)
     c_start(1)
     b_all_start(0)
-    eliminate(20, 42)
+    eliminate(16, 32)
     b_all_start(1)
     a_all_start(0)
-    eliminate(42, 50)
+    eliminate(32, 42)
     a_all_start(1)
-    eliminate(50, RANK)
+    eliminate(42, RANK)
     block(inverse_done)
-    core_all_start(0, False)
-    core_all_start(0, True)
+    core_all_start(0)
     block(p_sent)
-    block(w_sent, 0, SUMS)
-    block(w_sent, 1, SUMS)
-    core_all_start(1, False)
+    for n in range(NG):
+        block(w_sent, n, SUMS)
+    core_all_start(1)
     core_all_done(0)
     block(finish_gate)
-    block(w_sent, 0, (A_ALL, CORE_ALL))
-    core_all_start(1, True)
     core_all_done(1)
-    block(w_sent, 1, (A_ALL, CORE_ALL))
+    for n in range(NG):
+        block(w_sent, n, (A_ALL, CORE_ALL))
 
 
 def finish_kernel(
@@ -504,11 +510,12 @@
 
 
 def body(grad_gate, grad_up, err_gate, err_up, q_gate, q_up):
-    def part_scratch(*lead):
-        def of(divide, rows):
-            return [pltpu.VMEM(lead + (rows, width // divide), F32) for _, width in PARTS]
-
-        return of
+    def part_scratch(lead, rows, divide):
+        return [
+            pltpu.VMEM(lead + (rows, width // divide), F32)
+            for _, parts in GROUPS
+            for _, width, _ in parts
+        ]
 
     made = pl.pallas_call(
         exchange_kernel,
@@ -534,22 +541,22 @@
             pltpu.VMEM((2, RANK, HALF), F32),
             pltpu.VMEM((2, RANK, HALF), F32),
             pltpu.VMEM((2, RANK, HALF), F32),
-            *part_scratch(2, 3)(1, 16),
-            *part_scratch(2)(1, 16),
-            *part_scratch(2, 3)(2, 8),
-            *part_scratch(2, 4)(2, 8),
             pltpu.VMEM((RANK, 2 * RANK), F32),
             pltpu.VMEM((TENSOR, 8, 2 * RANK), F32),
             pltpu.VMEM((RANK, 2 * RANK), F32),
             pltpu.VMEM((RANK, 2 * RANK), F32),
             pltpu.VMEM((RANK, 2 * RANK), F32),
-            pltpu.SemaphoreType.DMA((2, CHUNKS, 3)),
+            pltpu.SemaphoreType.DMA((2, len(CHUNKS), 3)),
             pltpu.SemaphoreType.DMA((2, 2, 2)),
             pltpu.SemaphoreType.DMA((2, 2, 2)),
             pltpu.SemaphoreType.DMA((2,)),
             pltpu.SemaphoreType.DMA((2,)),
-            pltpu.SemaphoreType.DMA((2, 3, STAGES)),
-            pltpu.SemaphoreType.DMA((2, 3, STAGES)),
+            pltpu.SemaphoreType.DMA((NG, 3, STAGES)),
+            pltpu.SemaphoreType.DMA((NG, 3, STAGES)),
+            *part_scratch((3,), 16, 1),
+            *part_scratch((), 16, 1),
+            *part_scratch((3,), 8, 2),
+            *part_scratch((4,), 8, 2),
         ],
         compiler_params=pltpu.CompilerParams(
             collective_id=0, has_side_effects=True, vmem_limit_bytes=32 * 2**20

time: 59.6 us -> 56.9 us (0.955)
  Pallas kernels: 58.9 us -> 56 us
    pallas_call x1, Pallas kernels: 54.7 us -> 51.8 us  [body(): pl.pallas_call(exchange_kernel, out_shape=(pltpu.VMEM((ROWS, D), BF16), p...]
where the time goes in v5:
time: 56.9 us; the launch traced here: 56.8 us
  Pallas kernels  56 us (98%)
  between operations  0.8 us (1%)
    pallas_call x1, Pallas kernels, body(): pl.pallas_call(exchange_kernel, out_shape=(pltpu.VMEM((ROWS, D), BF16), p...  51.8 us
    pallas_call x1, Pallas kernels, body(): pl.pallas_call(finish_kernel, out_shape=(jax.ShapeDtypeStruct((ROWS, D),...  4.13 us

profile of v5, /device:TPU:1, one launch (start us, length us, event | category | flops | bytes accessed | tf_op | source)
XLA Modules:
  0.0 56.8 jit_solution(800039876229322385)
XLA Ops:
  0.6 51.8 %exchange.1 = (bf16[256,7168]{1,0:T(8,128)(2,1)S(1)}, f32[64,7168]{1,0:T(8,128)S(1)}, bf16[512,7168]{1,0:T(8,128)(2,1)S(1)}, f32[64,7168]{1,0:T(8,128)S(1)}, f32...) custom-call(bf16[256,7168]{1,0:T(8,128)(2,1)} %bitcast.10, bf16[256,7168]{1,0:T(8,128)(2,1)} %bitcast.11, ...), custom_call_target="tpu_custom_call" | custom-call | tf_op jit(solution)/shard_map/exchange/pallas_call | solution.py:520
  52.5 4.1 %finish.1 = (bf16[256,7168]{1,0:T(8,128)(2,1)}, bf16[256,7168]{1,0:T(8,128)(2,1)}, f32[64,7168]{1,0:T(8,128)}, f32[64,7168]{1,0:T(8,128)}) custom-call(bf16[256,7168]{1,0:T(8,128)(2,1)S(1)} %get-tuple-element.14.err_gate, f32[64,7168]{1,0:T(8,128)S(1)} %get-tuple-element.15.q_gate, bf16[512,7168]{1,0:T(8,128)(2,1)S(1)} %get-tuple-element.16.data, ...), custom_call_target="tpu_custom_call" | custom-call | tf_op jit(solution)/shard_map/finish/pallas_call | solution.py:575

commit v6 on v5

--- a/solution.py
+++ b/solution.py
@@ -241,13 +241,9 @@
                 half_part(w_send, n, p), half_part(w_recv, n, p), *sems(n, p, CORE_SUM), other_core
             )
 
-        def rest():
-            for p in range(3):
-                w_block(n, w_own, core, p)
-
         for p in range(3):
             block(other, p)
-        block(rest)
+        block(w_block, n, w_own, core, 0)
 
     def a_start(n):
         def step(p):
@@ -262,7 +258,9 @@
                     *sems(n, p, A_SUM), peer(a, v),
                 )
 
-        for p in range(3):
+        block(step, 0)
+        for p in (1, 2):
+            block(w_block, n, w_own, core, p)
             block(step, p)
 
     def b_start(n):

time: 56.9 us -> 56.3 us (0.989)
  Pallas kernels: 56 us -> 55.4 us
    pallas_call x1, Pallas kernels: 51.8 us -> 51.2 us  [body(): pl.pallas_call(exchange_kernel, out_shape=(pltpu.VMEM((ROWS, D), BF16), p...]
where the time goes in v6:
time: 56.3 us; the launch traced here: 56.2 us
  Pallas kernels  55.4 us (98%)
  between operations  0.8 us (1%)
    pallas_call x1, Pallas kernels, body(): pl.pallas_call(exchange_kernel, out_shape=(pltpu.VMEM((ROWS, D), BF16), p...  51.2 us
    pallas_call x1, Pallas kernels, body(): pl.pallas_call(finish_kernel, out_shape=(jax.ShapeDtypeStruct((ROWS, D),...  4.13 us

profile of v6, /device:TPU:1, one launch (start us, length us, event | category | flops | bytes accessed | tf_op | source)
XLA Modules:
  0.0 56.2 jit_solution(7378059097921193346)
XLA Ops:
  0.6 51.2 %exchange.1 = (bf16[256,7168]{1,0:T(8,128)(2,1)S(1)}, f32[64,7168]{1,0:T(8,128)S(1)}, bf16[512,7168]{1,0:T(8,128)(2,1)S(1)}, f32[64,7168]{1,0:T(8,128)S(1)}, f32...) custom-call(bf16[256,7168]{1,0:T(8,128)(2,1)} %bitcast.10, bf16[256,7168]{1,0:T(8,128)(2,1)} %bitcast.11, ...), custom_call_target="tpu_custom_call" | custom-call | tf_op jit(solution)/shard_map/exchange/pallas_call | solution.py:518
  51.9 4.1 %finish.1 = (bf16[256,7168]{1,0:T(8,128)(2,1)}, bf16[256,7168]{1,0:T(8,128)(2,1)}, f32[64,7168]{1,0:T(8,128)}, f32[64,7168]{1,0:T(8,128)}) custom-call(bf16[256,7168]{1,0:T(8,128)(2,1)S(1)} %get-tuple-element.14.err_gate, f32[64,7168]{1,0:T(8,128)S(1)} %get-tuple-element.15.q_gate, bf16[512,7168]{1,0:T(8,128)(2,1)S(1)} %get-tuple-element.16.data, ...), custom_call_target="tpu_custom_call" | custom-call | tf_op jit(solution)/shard_map/finish/pallas_call | solution.py:573

commit v7 on v6

--- a/solution.py
+++ b/solution.py
@@ -407,8 +407,10 @@
         diagonal = jnp.where(lane < RANK, gate, up)
         inverse[...] = low[...] / jnp.sqrt(diagonal)
 
+    def gate_stacks():
+        finish_stacks(inverse[:, :RANK], left[0], low_stack, ortho_stack)
+
     def finish_gate():
-        finish_stacks(inverse[:, :RANK], left[0], low_stack, ortho_stack)
         for i in range(BLOCKS):
             finish_block(
                 slice(i * BLOCK, (i + 1) * BLOCK), data_gate, total_gate, low_stack, ortho_stack,
@@ -460,6 +462,7 @@
     eliminate(42, RANK)
     block(inverse_done)
     core_all_start(0)
+    block(gate_stacks)
     block(p_sent)
     for n in range(NG):
         block(w_sent, n, SUMS)

time: 56.3 us -> 56.3 us (level)
  no operation moved by 1% of the time
where the time goes in v7:
time: 56.3 us; the launch traced here: 56.2 us
  Pallas kernels  55.4 us (98%)
  between operations  0.8 us (1%)
    pallas_call x1, Pallas kernels, body(): pl.pallas_call(exchange_kernel, out_shape=(pltpu.VMEM((ROWS, D), BF16), p...  51.2 us
    pallas_call x1, Pallas kernels, body(): pl.pallas_call(finish_kernel, out_shape=(jax.ShapeDtypeStruct((ROWS, D),...  4.13 us

profile of v7, /device:TPU:1, one launch (start us, length us, event | category | flops | bytes accessed | tf_op | source)
XLA Modules:
  0.0 56.2 jit_solution(11930780777069967120)
XLA Ops:
  0.6 51.2 %exchange.1 = (bf16[256,7168]{1,0:T(8,128)(2,1)S(1)}, f32[64,7168]{1,0:T(8,128)S(1)}, bf16[512,7168]{1,0:T(8,128)(2,1)S(1)}, f32[64,7168]{1,0:T(8,128)S(1)}, f32...) custom-call(bf16[256,7168]{1,0:T(8,128)(2,1)} %bitcast.10, bf16[256,7168]{1,0:T(8,128)(2,1)} %bitcast.11, ...), custom_call_target="tpu_custom_call" | custom-call | tf_op jit(solution)/shard_map/exchange/pallas_call | solution.py:521
  51.9 4.1 %finish.1 = (bf16[256,7168]{1,0:T(8,128)(2,1)}, bf16[256,7168]{1,0:T(8,128)(2,1)}, f32[64,7168]{1,0:T(8,128)}, f32[64,7168]{1,0:T(8,128)}) custom-call(bf16[256,7168]{1,0:T(8,128)(2,1)S(1)} %get-tuple-element.14.err_gate, f32[64,7168]{1,0:T(8,128)S(1)} %get-tuple-element.15.q_gate, bf16[512,7168]{1,0:T(8,128)(2,1)S(1)} %get-tuple-element.16.data, ...), custom_call_target="tpu_custom_call" | custom-call | tf_op jit(solution)/shard_map/finish/pallas_call | solution.py:576
